TPU v7x, 32 devices: a whole 2x2x4 slice. The times are simulated.
32 devices in a mesh: groups: 2 (over y), gz: 4 (over z), xy: 2 (over x), col: 2 (over core).
Axes of the slice: x: 2, y: 2, z: 4, core: 2. Of those that a mesh axis runs over, the one named last changes fastest.
Arguments:
- features: bfloat16 [8, 16, 256, 256], P(('groups', 'gz'), None, ('xy', 'col')), parts along dimension 0, may hold values from -24 to 24
- class_map: int32 [8, 256, 256], P(('groups', 'gz'), ('xy', 'col')), parts along dimension 0, may hold values from 0 to 3
- stiffness: float32 [4], replicated, may hold values from 0.2 to 2
- valid: int32 [8, 4], P('groups'), parts along dimension 0, may hold values 0 or 1
Outputs:
- displacement: float32 [8, 2, 256, 256], P(('groups', 'gz'), None, ('xy', 'col')), parts along dimension 0
- forward_flow: float32 [8, 2, 256, 256], P(('groups', 'gz'), None, ('xy', 'col')), parts along dimension 0
There are 2 independent parts, one for each index of `groups`. A program takes and returns all parts, laid end to end along the dimension named above; an argument that names none is the same for every part. Nothing has to cross between parts.
All inputs are finite; a program needn't handle non-finite values.
Results may differ from a plain program's by a relative error of at most 0.0017.
Values may be sent and summed in bfloat16 or wider, within the bound.
A program may use at most 64 MiB of HBM per device.

v0:
```python
import math

import jax
import jax.numpy as jnp
from jax import lax
from jax.sharding import PartitionSpec as P

RADIUS = 6
STEPS = 3


score_scale = 0.25
step_size = 0.1
saturation = 2.0


def padded_2(cells, sides, width):
    for axis, dim in sides:
        count = lax.axis_size(axis)
        ends = count - 1
        head = lax.slice_in_dim(cells, 0, width, axis=dim)
        tail = lax.slice_in_dim(cells, cells.shape[dim] - width, cells.shape[dim], axis=dim)
        cells = jnp.concatenate(
            [
                lax.ppermute(tail, axis, [(i, (i + 1) % count) for i in range(ends)]),
                cells,
                lax.ppermute(head, axis, [((i + 1) % count, i) for i in range(ends)]),
            ],
            axis=dim,
        )
    return cells


def passed_along(value, axis, steps):
    count = lax.axis_size(axis)
    initial, last = (max(0, -steps), min(count, count - steps))
    return lax.ppermute(value, axis, [(source, source + steps) for source in range(initial, last)])


def entering(shard, axis, combine, identity):
    length, here = (lax.axis_size(axis), lax.axis_index(axis))
    everything = lax.all_gather(shard, axis)
    start = jnp.broadcast_to(jnp.asarray(identity, shard.dtype), shard.shape)

    def step(k, before):
        reached = k < here
        new = combine(before, everything[k])
        return jnp.where(reached, new, before)

    return lax.fori_loop(0, length, step, start)


def shortened(shard):
    return jax.tree.map(lambda a: a.astype(jnp.bfloat16) if a.dtype == jnp.float32 else a, shard)


def expected(stacked):
    highest = jnp.max(stacked, axis=0)
    weights = jnp.exp(stacked - highest)
    denominator = jnp.sum(weights, axis=0)
    window = 2 * RADIUS + 1
    places = jnp.arange(window * window, dtype=jnp.int32)
    row_shift = (places // window - RADIUS).astype(jnp.float32)
    col_shift = (places % window - RADIUS).astype(jnp.float32)
    flow_row = jnp.sum(weights * row_shift[:, None, None], axis=0) / denominator
    flow_col = jnp.sum(weights * col_shift[:, None, None], axis=0) / denominator
    return jnp.stack([flow_row, flow_col])


def band_scores(center_band, window_band, height, breadth):
    scores = []
    for shift_row in range(2 * RADIUS + 1):
        for shift_col in range(2 * RADIUS + 1):
            scores.append(
                jnp.sum(
                    center_band
                    * window_band[
                        :, shift_row : shift_row + height, shift_col : shift_col + breadth
                    ],
                    axis=0,
                )
            )
    return score_scale * jnp.stack(scores)


def flow_of(center, other):
    channels, height, breadth = center.shape
    band_rows = math.gcd(height, 16)

    def one_band(band_index):
        band_start = band_index * band_rows
        center_band = lax.dynamic_slice_in_dim(center, band_start, band_rows, 1).astype(jnp.float32)
        window_band = lax.dynamic_slice_in_dim(other, band_start, band_rows + 2 * RADIUS, 1).astype(
            jnp.float32
        )
        return expected(band_scores(center_band, window_band, band_rows, breadth))

    results = lax.map(one_band, jnp.arange(height // band_rows, dtype=jnp.int32))
    return jnp.moveaxis(results, 0, 1).reshape(2, height, breadth)


def widen(values_in, margin):
    padding = [(0, 0)] * (values_in.ndim - 1) + [(margin, margin)]
    return jnp.pad(values_in, padding)


def elastic_term(disp_pad, stiff_pad):
    middle = disp_pad[..., 1:-1, 1:-1]
    stiff_mid = stiff_pad[..., 1:-1, 1:-1]
    result = jnp.zeros_like(middle)
    for row_part, col_part in (
        (slice(2, None), slice(1, -1)),
        (slice(0, -2), slice(1, -1)),
        (slice(1, -1), slice(2, None)),
        (slice(1, -1), slice(0, -2)),
    ):
        neighbour_stiff = stiff_pad[..., row_part, col_part]
        result = result + 0.5 * (stiff_mid + neighbour_stiff) * (
            middle - disp_pad[..., row_part, col_part]
        )
    return result


def spring(vector):
    return vector / jnp.sqrt(
        1.0 + jnp.sum(vector * vector, axis=-3, keepdims=True) / (saturation * saturation)
    )


def add_pair(earlier, later):
    return earlier + later


def on_device(features, class_map, stiffness, valid):
    center = features[0]
    height, breadth = (center.shape[1], center.shape[2])
    section = lax.axis_index("gz")
    tile_index = lax.axis_index(("xy", "col"))
    column = lax.dynamic_slice_in_dim(valid, tile_index, 1, 1)[:, 0].astype(jnp.float32)
    link_all = column * jnp.concatenate([column[1:], jnp.zeros((1,), jnp.float32)])
    link_here = lax.dynamic_index_in_dim(link_all, section, 0, keepdims=False)
    link_below = jnp.where(
        section > 0,
        lax.dynamic_index_in_dim(link_all, jnp.maximum(section - 1, 0), 0, keepdims=False),
        0.0,
    )
    padded = widen(padded_2(center, ((("xy", "col"), 1),), RADIUS), RADIUS)
    upper_pad = passed_along(padded, "gz", -1)
    forward = flow_of(center, upper_pad)
    ahead_flow = flow_of(upper_pad[:, RADIUS : RADIUS + height, RADIUS : RADIUS + breadth], padded)
    passed = passed_along(jnp.stack([forward, ahead_flow]), "gz", 1)
    prior_flow = passed[0]
    backward = passed[1]
    excess = link_here * forward - link_below * backward
    before = entering(excess, "gz", add_pair, jnp.zeros_like(excess))
    displace = 0.5 * (before - link_below * backward)
    levels = jnp.arange(stiffness.shape[0], dtype=jnp.int32)
    stiff_field = jnp.sum(
        jnp.where(class_map[0][None] == levels[:, None, None], stiffness[:, None, None], 0.0),
        axis=0,
    )
    stiff_pad = widen(padded_2(stiff_field, ((("xy", "col"), 0),), 1), 1)
    for step_number in range(STEPS):
        disp_pad = widen(padded_2(displace, ((("xy", "col"), 1),), 1), 1)
        elastic = elastic_term(disp_pad, stiff_pad)
        upper_disp = passed_along(shortened(displace), "gz", -1).astype(displace.dtype)
        lower_disp = passed_along(shortened(displace), "gz", 1).astype(displace.dtype)
        pull_up = link_here * spring(upper_disp - displace - forward)
        pull_down = link_below * spring(lower_disp - displace - backward)
        from_below = link_below * spring(displace - lower_disp - prior_flow)
        from_above = link_here * spring(displace - upper_disp - ahead_flow)
        gradient = elastic - pull_up - pull_down + from_below + from_above
        displace = displace - step_size * gradient
    return (displace[None], forward[None])


def solution(mesh):
    placed = (
        P(("groups", "gz"), None, ("xy", "col"), None),
        P(("groups", "gz"), ("xy", "col"), None),
        P(),
        P("groups", None),
    )
    return jax.shard_map(
        on_device,
        mesh=mesh,
        in_specs=placed,
        out_specs=(
            P(("groups", "gz"), None, ("xy", "col"), None),
            P(("groups", "gz"), None, ("xy", "col"), None),
        ),
        check_vma=False,
    )
```

profile of v0, /device:TPU:9, one launch (start us, length us, event | category | flops | bytes accessed | tf_op | source)
XLA Modules:
  0.0 259.5 jit_solution(13074941978492114994)
XLA Ops:
  0.7 1.4 copy.204
  2.0 2.6 collective-permute-start.1
  4.6 3.0 %collective-permute-start = (bf16[16,6,256]{2,0,1:T(8,128)(2,1)S(1)}, bf16[16,6,256]{2,0,1:T(8,128)(2,1)S(1)}, u32[]{:S(2)}, u32[]{:S(2)}) collective-permute-start(bf16[16,6,256]{2,0,1:T(8,128)(2,1)S(1)} %get-tuple-element.723), channel_id=1, source_target_pairs={{0,1},{1,2},{2,3},{4,5},{5,6},{6,7},{8,9},{9,10},{10,11},{12,13},{... | collective-permute-start | bytes 147464 | tf_op jit(solution)/shard_map/ppermute | solution.py:25
  9.3 2.1 collective-permute-start.2
  12.7 1.9 collective-permute-start.4
  14.6 4.5 %collective-permute-start.6 = (f32[1,256]{1,0:T(1,128)}, f32[1,256]{1,0:T(1,128)}, u32[]{:S(2)}, u32[]{:S(2)}) collective-permute-start(f32[1,256]{1,0:T(1,128)} %get-tuple-element.735), channel_id=1, source_target_pairs={{0,1},{1,2},{2,3},{4,5},{5,6},{6,7},{8,9},{9,10},{10,11},{12,13},{... | collective-permute-start | bytes 3080 | tf_op jit(solution)/shard_map/ppermute | solution.py:25
  20.5 12.6 %collective-permute-done.2 = bf16[16,76,268]{2,0,1:T(8,128)(2,1)S(1)} collective-permute-done((bf16[16,76,268]{2,0,1:T(8,128)(2,1)S(1)}, bf16[16,76,268]{2,0,1:T(8,128)(2,1)S(1)}, u32[]{:S(2)}, u32[]{:S(2)}) %collective-permute-start.2) | collective-permute-done | bytes 651808 | tf_op jit(solution)/shard_map/ppermute | solution.py:37
  33.2 91.1 %while.40 = (s32[]{:T(128)}, f32[4,2,16,256]{3,2,1,0:T(8,128)S(1)}, s32[4]{0:T(128)S(1)}, bf16[16,64,256]{2,1,0:T(8,128)(2,1)}, bf16[16,76,268]{2,0,1:T(8,128)(2...) while((s32[]{:T(128)}, f32[4,2,16,256]{3,2,1,0:T(8,128)S(1)}, ...), condition=%wide.region_174.175_spmd, body=%wide.region_0.174_spmd.sunk | while | flops 28467096 | bytes 62987676 | solution.py:98
  34.7 2.0 fusion.465
  38.2 2.1 fusion.467
  40.4 2.1 fusion.468
  42.7 2.1 fusion.469
  45.0 2.0 fusion.470
  47.3 2.1 fusion.471
  49.5 2.1 fusion.472
  57.5 2.0 fusion.465
  60.9 2.1 fusion.467
  63.2 2.1 fusion.468
  65.5 2.1 fusion.469
  67.8 2.0 fusion.470
  70.0 2.1 fusion.471
  72.3 2.1 fusion.472
  80.3 2.0 fusion.465
  83.7 2.1 fusion.467
  86.0 2.1 fusion.468
  88.3 2.1 fusion.469
  90.6 2.0 fusion.470
  92.8 2.1 fusion.471
  95.1 2.1 fusion.472
  103.1 2.0 fusion.465
  106.5 2.1 fusion.467
  108.8 2.1 fusion.468
  111.1 2.1 fusion.469
  113.4 2.0 fusion.470
  115.6 2.1 fusion.471
  117.9 2.1 fusion.472
  124.7 65.4 %while.41 = (s32[]{:T(128)}, f32[4,2,16,256]{3,2,1,0:T(8,128)S(1)}, s32[4]{0:T(128)S(1)}, bf16[16,64,256]{2,0,1:T(8,128)(2,1)S(1)}, bf16[16,76,268]{2,0,1:T(8,12...) while((s32[]{:T(128)}, f32[4,2,16,256]{3,2,1,0:T(8,128)S(1)}, ...), condition=%wide.region_349.350_spmd, body=%wide.region_175.349_spmd.sunk | while | flops 28467096 | bytes 61152604 | solution.py:98
  135.4 1.2 fusion.484
  136.9 1.2 fusion.485
  138.3 1.2 fusion.486
  151.6 1.2 fusion.484
  153.1 1.2 fusion.485
  154.5 1.2 fusion.486
  169.4 1.2 fusion.485
  185.6 1.2 fusion.485
  190.1 3.2 %collective-permute-start.3 = (f32[2,2,64,256]{3,2,1,0:T(8,128)S(1)}, f32[2,2,64,256]{3,2,1,0:T(8,128)S(1)}, u32[]{:S(2)}, u32[]{:S(2)}) collective-permute-start(f32[2,2,64,256]{3,2,1,0:T(8,128)S(1)} %pad_maximum_fusion), channel_id=1, source_target_pairs={{0,4},{4,8},{8,12},{1,5},{5,9},{9,13},{2,6},{6,10},{10,14},{3,7},{... | collective-permute-start | bytes 786440 | tf_op jit(solution)/shard_map/ppermute | solution.py:37
  195.6 4.0 %collective-permute-done.3 = f32[2,2,64,256]{3,2,1,0:T(8,128)S(1)} collective-permute-done((f32[2,2,64,256]{3,2,1,0:T(8,128)S(1)}, f32[2,2,64,256]{3,2,1,0:T(8,128)S(1)}, u32[]{:S(2)}, u32[]{:S(2)}) %collective-permute-start.3) | collective-permute-done | bytes 262176 | tf_op jit(solution)/shard_map/ppermute | solution.py:37
  200.2 11.5 %all_gather.4 = f32[4,2,64,256]{3,2,1,0:T(8,128)S(1)} all-gather(f32[1,2,64,256]{3,2,1,0:T(8,128)S(1)} %multiply_subtract_fusion), channel_id=1, replica_groups=mesh['groups'=2,'gz'=4,'xy'=2,'col'=2] {'gz'}, dimensions={0}, use_global_device_ids=true | all-gather | bytes 655360 | tf_op jit(solution)/shard_map/all_gather | solution.py:42
  212.0 6.2 %collective-permute-start.5 = (f32[2,1,256]{2,1,0:T(1,128)S(1)}, f32[2,1,256]{2,1,0:T(1,128)S(1)}, u32[]{:S(2)}, u32[]{:S(2)}) collective-permute-start(f32[2,1,256]{2,1,0:T(1,128)S(1)} %get-tuple-element.732), channel_id=1, source_target_pairs={{1,0},{2,1},{3,2},{5,4},{6,5},{7,6},{9,8},{10,9},{11,10},{13,12},{... | collective-permute-start | bytes 6152 | tf_op jit(solution)/shard_map/ppermute | solution.py:27
  218.2 1.9 collective-permute-start.7
  220.9 2.7 %collective-permute-start.8 = (bf16[2,64,256]{2,1,0:T(8,128)(2,1)S(1)}, bf16[2,64,256]{2,1,0:T(8,128)(2,1)S(1)}, u32[]{:S(2)}, u32[]{:S(2)}) collective-permute-start(bf16[2,64,256]{2,1,0:T(8,128)(2,1)S(1)} %get-tuple-element.699), channel_id=1, source_target_pairs={{4,0},{8,4},{12,8},{5,1},{9,5},{13,9},{6,2},{10,6},{14,10},{7,3},{... | collective-permute-start | bytes 196616 | tf_op jit(solution)/shard_map/ppermute | solution.py:37
  223.7 2.6 collective-permute-start.9
  226.4 2.3 collective-permute-done.9
  229.8 3.8 %collective-permute-start.10 = (f32[2,1,256]{2,1,0:T(1,128)S(1)}, f32[2,1,256]{2,1,0:T(1,128)S(1)}, u32[]{:S(2)}, u32[]{:S(2)}) collective-permute-start(f32[2,1,256]{2,1,0:T(1,128)S(1)} %get-tuple-element.730), channel_id=1, source_target_pairs={{1,0},{2,1},{3,2},{5,4},{6,5},{7,6},{9,8},{10,9},{11,10},{13,12},{... | collective-permute-start | bytes 6152 | tf_op jit(solution)/shard_map/ppermute | solution.py:27
  233.6 1.9 collective-permute-start.11
  235.5 1.9 collective-permute-start.12
  237.4 3.4 %collective-permute-start.13 = (bf16[2,64,256]{2,1,0:T(8,128)(2,1)S(1)}, bf16[2,64,256]{2,1,0:T(8,128)(2,1)S(1)}, u32[]{:S(2)}, u32[]{:S(2)}) collective-permute-start(bf16[2,64,256]{2,1,0:T(8,128)(2,1)S(1)} %get-tuple-element.697), channel_id=1, source_target_pairs={{0,4},{4,8},{8,12},{1,5},{5,9},{9,13},{2,6},{6,10},{10,14},{3,7},{... | collective-permute-start | bytes 196616 | tf_op jit(solution)/shard_map/ppermute | solution.py:37
  241.0 1.5 collective-permute-done.13
  243.6 3.6 %collective-permute-start.14 = (f32[2,1,256]{2,1,0:T(1,128)S(1)}, f32[2,1,256]{2,1,0:T(1,128)S(1)}, u32[]{:S(2)}, u32[]{:S(2)}) collective-permute-start(f32[2,1,256]{2,1,0:T(1,128)S(1)} %get-tuple-element.728), channel_id=1, source_target_pairs={{1,0},{2,1},{3,2},{5,4},{6,5},{7,6},{9,8},{10,9},{11,10},{13,12},{... | collective-permute-start | bytes 6152 | tf_op jit(solution)/shard_map/ppermute | solution.py:27
  247.1 2.0 collective-permute-start.15
  249.1 3.6 %collective-permute-start.17 = (bf16[2,64,256]{2,1,0:T(8,128)(2,1)S(1)}, bf16[2,64,256]{2,1,0:T(8,128)(2,1)S(1)}, u32[]{:S(2)}, u32[]{:S(2)}) collective-permute-start(bf16[2,64,256]{2,1,0:T(8,128)(2,1)S(1)} %get-tuple-element.695), channel_id=1, source_target_pairs={{0,4},{4,8},{8,12},{1,5},{5,9},{9,13},{2,6},{6,10},{10,14},{3,7},{... | collective-permute-start | bytes 196616 | tf_op jit(solution)/shard_map/ppermute | solution.py:37
  252.7 1.9 collective-permute-start.16
  254.8 2.9 %collective-permute-done.16 = bf16[2,64,256]{2,1,0:T(8,128)(2,1)S(1)} collective-permute-done((bf16[2,64,256]{2,1,0:T(8,128)(2,1)S(1)}, bf16[2,64,256]{2,1,0:T(8,128)(2,1)S(1)}, u32[]{:S(2)}, u32[]{:S(2)}) %collective-permute-start.16) | collective-permute-done | bytes 65568 | tf_op jit(solution)/shard_map/ppermute | solution.py:37
  258.0 1.5 fusion.381
  (1548 shorter events, 81.9 us)
Async XLA Ops:
  0.6 10.8 %copy-start.8 = (f32[4]{0:T(128)S(1)}, f32[4]{0:T(128)}, u32[]{:S(2)}) copy-start(f32[4]{0:T(128)} %param.12) | copy-start | bytes 52
  0.6 10.8 %copy-start.4 = (s32[1,64,256]{2,1,0:T(8,128)S(1)}, s32[1,64,256]{2,1,0:T(8,128)}, u32[]{:S(2)}) copy-start(s32[1,64,256]{2,1,0:T(8,128)} %param.11) | copy-start | bytes 196612
  0.7 18.5 %copy-start.5 = (s32[4,4]{1,0:T(4,128)S(1)}, s32[4,4]{1,0:T(4,128)}, u32[]{:S(2)}) copy-start(s32[4,4]{1,0:T(4,128)} %param.13) | copy-start | bytes 196
  2.0 5.6 %collective-permute-start.1 = (bf16[16,6,256]{2,0,1:T(8,128)(2,1)S(1)}, bf16[16,6,256]{2,0,1:T(8,128)(2,1)S(1)}, u32[]{:S(2)}, u32[]{:S(2)}) collective-permute-start(bf16[16,6,256]{2,0,1:T(8,128)(2,1)S(1)} %get-tuple-element.724), channel_id=1, source_target_pairs={{1,0},{2,1},{3,2},{5,4},{6,5},{7,6},{9,8},{10,9},{11,10},{13,12},{... | collective-permute-start | bytes 147464 | tf_op jit(solution)/shard_map/ppermute | solution.py:27
  4.6 4.2 %collective-permute-start = (bf16[16,6,256]{2,0,1:T(8,128)(2,1)S(1)}, bf16[16,6,256]{2,0,1:T(8,128)(2,1)S(1)}, u32[]{:S(2)}, u32[]{:S(2)}) collective-permute-start(bf16[16,6,256]{2,0,1:T(8,128)(2,1)S(1)} %get-tuple-element.723), channel_id=1, source_target_pairs={{0,1},{1,2},{2,3},{4,5},{5,6},{6,7},{8,9},{9,10},{10,11},{12,13},{... | collective-permute-start | bytes 147464 | tf_op jit(solution)/shard_map/ppermute | solution.py:25
  9.3 23.9 %collective-permute-start.2 = (bf16[16,76,268]{2,0,1:T(8,128)(2,1)S(1)}, bf16[16,76,268]{2,0,1:T(8,128)(2,1)S(1)}, u32[]{:S(2)}, u32[]{:S(2)}) collective-permute-start(bf16[16,76,268]{2,0,1:T(8,128)(2,1)S(1)} %fusion.359), channel_id=1, source_target_pairs={{4,0},{8,4},{12,8},{5,1},{9,5},{13,9},{6,2},{10,6},{14,10},{7,3},{... | collective-permute-start | bytes 1955336 | tf_op jit(solution)/shard_map/ppermute | solution.py:37
  11.5 0.6 copy-start.2
  12.7 182.1 %collective-permute-start.4 = (f32[1,256]{1,0:T(1,128)}, f32[1,256]{1,0:T(1,128)}, u32[]{:S(2)}, u32[]{:S(2)}) collective-permute-start(f32[1,256]{1,0:T(1,128)} %get-tuple-element.736), channel_id=1, source_target_pairs={{1,0},{2,1},{3,2},{5,4},{6,5},{7,6},{9,8},{10,9},{11,10},{13,12},{... | collective-permute-start | bytes 3080 | tf_op jit(solution)/shard_map/ppermute | solution.py:27
  14.6 180.2 %collective-permute-start.6 = (f32[1,256]{1,0:T(1,128)}, f32[1,256]{1,0:T(1,128)}, u32[]{:S(2)}, u32[]{:S(2)}) collective-permute-start(f32[1,256]{1,0:T(1,128)} %get-tuple-element.735), channel_id=1, source_target_pairs={{0,1},{1,2},{2,3},{4,5},{5,6},{6,7},{8,9},{9,10},{10,11},{12,13},{... | collective-permute-start | bytes 3080 | tf_op jit(solution)/shard_map/ppermute | solution.py:25
  34.6 2.2 copy-start
  57.4 2.2 copy-start
  80.2 2.2 copy-start
  103.0 2.2 copy-start
  124.4 133.6 %copy-start.1 = (f32[2,4,16,256]{3,2,1,0:T(8,128)}, f32[2,4,16,256]{3,2,1,0:T(8,128)S(1)}, u32[]{:S(2)}) copy-start(f32[2,4,16,256]{3,2,1,0:T(8,128)S(1)} %copy.22) | copy-start | bytes 393220
  124.6 68.7 %copy-start.6 = (f32[4]{0:T(128)S(1)}, f32[4]{0:T(128)}, u32[]{:S(2)}) copy-start(f32[4]{0:T(128)} %get-tuple-element.701) | copy-start | bytes 52
  124.6 68.7 %copy-start.7 = (f32[3]{0:T(128)S(1)}, f32[3]{0:T(128)}, u32[]{:S(2)}) copy-start(f32[3]{0:T(128)} %slice_reduce_fusion) | copy-start | bytes 40
  124.7 70.2 %copy-start.3 = (f32[64,256]{1,0:T(8,128)S(1)}, f32[64,256]{1,0:T(8,128)}, u32[]{:S(2)}) copy-start(f32[64,256]{1,0:T(8,128)} %copy-done.2) | copy-start | bytes 196612
  190.1 9.5 %collective-permute-start.3 = (f32[2,2,64,256]{3,2,1,0:T(8,128)S(1)}, f32[2,2,64,256]{3,2,1,0:T(8,128)S(1)}, u32[]{:S(2)}, u32[]{:S(2)}) collective-permute-start(f32[2,2,64,256]{3,2,1,0:T(8,128)S(1)} %pad_maximum_fusion), channel_id=1, source_target_pairs={{0,4},{4,8},{8,12},{1,5},{5,9},{9,13},{2,6},{6,10},{10,14},{3,7},{... | collective-permute-start | bytes 786440 | tf_op jit(solution)/shard_map/ppermute | solution.py:37
  212.0 14.2 %collective-permute-start.5 = (f32[2,1,256]{2,1,0:T(1,128)S(1)}, f32[2,1,256]{2,1,0:T(1,128)S(1)}, u32[]{:S(2)}, u32[]{:S(2)}) collective-permute-start(f32[2,1,256]{2,1,0:T(1,128)S(1)} %get-tuple-element.732), channel_id=1, source_target_pairs={{1,0},{2,1},{3,2},{5,4},{6,5},{7,6},{9,8},{10,9},{11,10},{13,12},{... | collective-permute-start | bytes 6152 | tf_op jit(solution)/shard_map/ppermute | solution.py:27
  218.2 8.0 %collective-permute-start.7 = (f32[2,1,256]{2,1,0:T(1,128)S(1)}, f32[2,1,256]{2,1,0:T(1,128)S(1)}, u32[]{:S(2)}, u32[]{:S(2)}) collective-permute-start(f32[2,1,256]{2,1,0:T(1,128)S(1)} %get-tuple-element.731), channel_id=1, source_target_pairs={{0,1},{1,2},{2,3},{4,5},{5,6},{6,7},{8,9},{9,10},{10,11},{12,13},{... | collective-permute-start | bytes 6152 | tf_op jit(solution)/shard_map/ppermute | solution.py:25
  220.9 5.5 %collective-permute-start.8 = (bf16[2,64,256]{2,1,0:T(8,128)(2,1)S(1)}, bf16[2,64,256]{2,1,0:T(8,128)(2,1)S(1)}, u32[]{:S(2)}, u32[]{:S(2)}) collective-permute-start(bf16[2,64,256]{2,1,0:T(8,128)(2,1)S(1)} %get-tuple-element.699), channel_id=1, source_target_pairs={{4,0},{8,4},{12,8},{5,1},{9,5},{13,9},{6,2},{10,6},{14,10},{7,3},{... | collective-permute-start | bytes 196616 | tf_op jit(solution)/shard_map/ppermute | solution.py:37
  223.7 5.0 %collective-permute-start.9 = (bf16[2,64,256]{2,1,0:T(8,128)(2,1)S(1)}, bf16[2,64,256]{2,1,0:T(8,128)(2,1)S(1)}, u32[]{:S(2)}, u32[]{:S(2)}) collective-permute-start(bf16[2,64,256]{2,1,0:T(8,128)(2,1)S(1)} %get-tuple-element.699), channel_id=1, source_target_pairs={{0,4},{4,8},{8,12},{1,5},{5,9},{9,13},{2,6},{6,10},{10,14},{3,7},{... | collective-permute-start | bytes 196616 | tf_op jit(solution)/shard_map/ppermute | solution.py:37
  229.8 11.1 %collective-permute-start.10 = (f32[2,1,256]{2,1,0:T(1,128)S(1)}, f32[2,1,256]{2,1,0:T(1,128)S(1)}, u32[]{:S(2)}, u32[]{:S(2)}) collective-permute-start(f32[2,1,256]{2,1,0:T(1,128)S(1)} %get-tuple-element.730), channel_id=1, source_target_pairs={{1,0},{2,1},{3,2},{5,4},{6,5},{7,6},{9,8},{10,9},{11,10},{13,12},{... | collective-permute-start | bytes 6152 | tf_op jit(solution)/shard_map/ppermute | solution.py:27
  233.6 7.2 %collective-permute-start.11 = (f32[2,1,256]{2,1,0:T(1,128)S(1)}, f32[2,1,256]{2,1,0:T(1,128)S(1)}, u32[]{:S(2)}, u32[]{:S(2)}) collective-permute-start(f32[2,1,256]{2,1,0:T(1,128)S(1)} %get-tuple-element.729), channel_id=1, source_target_pairs={{0,1},{1,2},{2,3},{4,5},{5,6},{6,7},{8,9},{9,10},{10,11},{12,13},{... | collective-permute-start | bytes 6152 | tf_op jit(solution)/shard_map/ppermute | solution.py:25
  235.5 5.5 %collective-permute-start.12 = (bf16[2,64,256]{2,1,0:T(8,128)(2,1)S(1)}, bf16[2,64,256]{2,1,0:T(8,128)(2,1)S(1)}, u32[]{:S(2)}, u32[]{:S(2)}) collective-permute-start(bf16[2,64,256]{2,1,0:T(8,128)(2,1)S(1)} %get-tuple-element.697), channel_id=1, source_target_pairs={{4,0},{8,4},{12,8},{5,1},{9,5},{13,9},{6,2},{10,6},{14,10},{7,3},{... | collective-permute-start | bytes 196616 | tf_op jit(solution)/shard_map/ppermute | solution.py:37
  237.4 5.0 %collective-permute-start.13 = (bf16[2,64,256]{2,1,0:T(8,128)(2,1)S(1)}, bf16[2,64,256]{2,1,0:T(8,128)(2,1)S(1)}, u32[]{:S(2)}, u32[]{:S(2)}) collective-permute-start(bf16[2,64,256]{2,1,0:T(8,128)(2,1)S(1)} %get-tuple-element.697), channel_id=1, source_target_pairs={{0,4},{4,8},{8,12},{1,5},{5,9},{9,13},{2,6},{6,10},{10,14},{3,7},{... | collective-permute-start | bytes 196616 | tf_op jit(solution)/shard_map/ppermute | solution.py:37
  243.6 11.1 %collective-permute-start.14 = (f32[2,1,256]{2,1,0:T(1,128)S(1)}, f32[2,1,256]{2,1,0:T(1,128)S(1)}, u32[]{:S(2)}, u32[]{:S(2)}) collective-permute-start(f32[2,1,256]{2,1,0:T(1,128)S(1)} %get-tuple-element.728), channel_id=1, source_target_pairs={{1,0},{2,1},{3,2},{5,4},{6,5},{7,6},{9,8},{10,9},{11,10},{13,12},{... | collective-permute-start | bytes 6152 | tf_op jit(solution)/shard_map/ppermute | solution.py:27
  247.1 7.5 %collective-permute-start.15 = (f32[2,1,256]{2,1,0:T(1,128)S(1)}, f32[2,1,256]{2,1,0:T(1,128)S(1)}, u32[]{:S(2)}, u32[]{:S(2)}) collective-permute-start(f32[2,1,256]{2,1,0:T(1,128)S(1)} %get-tuple-element.727), channel_id=1, source_target_pairs={{0,1},{1,2},{2,3},{4,5},{5,6},{6,7},{8,9},{9,10},{10,11},{12,13},{... | collective-permute-start | bytes 6152 | tf_op jit(solution)/shard_map/ppermute | solution.py:25
  249.1 5.7 %collective-permute-start.17 = (bf16[2,64,256]{2,1,0:T(8,128)(2,1)S(1)}, bf16[2,64,256]{2,1,0:T(8,128)(2,1)S(1)}, u32[]{:S(2)}, u32[]{:S(2)}) collective-permute-start(bf16[2,64,256]{2,1,0:T(8,128)(2,1)S(1)} %get-tuple-element.695), channel_id=1, source_target_pairs={{0,4},{4,8},{8,12},{1,5},{5,9},{9,13},{2,6},{6,10},{10,14},{3,7},{... | collective-permute-start | bytes 196616 | tf_op jit(solution)/shard_map/ppermute | solution.py:37
  252.7 5.0 %collective-permute-start.16 = (bf16[2,64,256]{2,1,0:T(8,128)(2,1)S(1)}, bf16[2,64,256]{2,1,0:T(8,128)(2,1)S(1)}, u32[]{:S(2)}, u32[]{:S(2)}) collective-permute-start(bf16[2,64,256]{2,1,0:T(8,128)(2,1)S(1)} %get-tuple-element.695), channel_id=1, source_target_pairs={{4,0},{8,4},{12,8},{5,1},{9,5},{13,9},{6,2},{10,6},{14,10},{7,3},{... | collective-permute-start | bytes 196616 | tf_op jit(solution)/shard_map/ppermute | solution.py:37
where the time goes:
time: 263 us; the launch traced here: 259 us
  other arithmetic  136 us (52%)
  starting transfers between devices  52.8 us (20%)
  waiting for transfers between devices  24.4 us (9%)
  loops' own time  18 us (7%)
  local copies, waits for them, and re-layouts  14.9 us (6%)
  blocking collectives  11.5 us (4%)
    reduce_sum x80, other arithmetic, band_scores(): jnp.sum(center_band * window_band[:, shift_row:shift_row + height, shift_...  117 us
    ppermute x8, waiting for transfers between devices, passed_along(): lax.ppermute(value, axis, [(source, source + steps) for source in range(i...  23.2 us
    ppermute x8, starting transfers between devices, passed_along(): lax.ppermute(value, axis, [(source, source + steps) for source in range(i...  21.3 us
    ppermute x5, starting transfers between devices, padded_2(): lax.ppermute(head, axis, [((i + 1) % count, i) for i in range(ends)])  18.1 us
    another operation x2, loops' own time, flow_of(): lax.map(one_band, jnp.arange(height // band_rows, dtype=jnp.int32))  17.9 us
    ppermute x5, starting transfers between devices, padded_2(): lax.ppermute(tail, axis, [(i, (i + 1) % count) for i in range(ends)])  13.4 us
    all_gather x1, blocking collectives, entering(): everything = lax.all_gather(shard, axis)  11.5 us
    reduce_sum x8, other arithmetic, expected(): flow_row = jnp.sum(weights * row_shift[:, None, None], axis=0) / denominator  8.45 us
  transfers between devices with their start and end apart: 18, of which 6 were waited for; matrix products, arithmetic and copies ran while one was open for 55% of the time, Pallas kernels for 0%

commit v1 on v0

--- a/solution.py
+++ b/solution.py
@@ -3,6 +3,8 @@
 import jax
 import jax.numpy as jnp
 from jax import lax
+from jax.experimental import pallas as pl
+from jax.experimental.pallas import tpu as pltpu
 from jax.sharding import PartitionSpec as P
 
 RADIUS = 6
@@ -37,66 +39,178 @@
     return lax.ppermute(value, axis, [(source, source + steps) for source in range(initial, last)])
 
 
-def entering(shard, axis, combine, identity):
-    length, here = (lax.axis_size(axis), lax.axis_index(axis))
-    everything = lax.all_gather(shard, axis)
-    start = jnp.broadcast_to(jnp.asarray(identity, shard.dtype), shard.shape)
-
-    def step(k, before):
-        reached = k < here
-        new = combine(before, everything[k])
-        return jnp.where(reached, new, before)
-
-    return lax.fori_loop(0, length, step, start)
-
-
 def shortened(shard):
     return jax.tree.map(lambda a: a.astype(jnp.bfloat16) if a.dtype == jnp.float32 else a, shard)
 
 
-def expected(stacked):
-    highest = jnp.max(stacked, axis=0)
-    weights = jnp.exp(stacked - highest)
-    denominator = jnp.sum(weights, axis=0)
-    window = 2 * RADIUS + 1
-    places = jnp.arange(window * window, dtype=jnp.int32)
-    row_shift = (places // window - RADIUS).astype(jnp.float32)
-    col_shift = (places % window - RADIUS).astype(jnp.float32)
-    flow_row = jnp.sum(weights * row_shift[:, None, None], axis=0) / denominator
-    flow_col = jnp.sum(weights * col_shift[:, None, None], axis=0) / denominator
-    return jnp.stack([flow_row, flow_col])
-
-
-def band_scores(center_band, window_band, height, breadth):
-    scores = []
-    for shift_row in range(2 * RADIUS + 1):
-        for shift_col in range(2 * RADIUS + 1):
-            scores.append(
-                jnp.sum(
-                    center_band
-                    * window_band[
-                        :, shift_row : shift_row + height, shift_col : shift_col + breadth
-                    ],
-                    axis=0,
+LANES = 128
+EDGE = 8
+SPAN = 2 * RADIUS + 1
+
+
+def shifted(halves, amount, lane):
+    count = len(halves)
+    source = lane - amount
+    turned = [pltpu.roll(half, lax.rem(amount + LANES, LANES), 1) for half in halves]
+    blank = jnp.zeros_like(turned[0])
+    inside = (source >= 0) & (source < LANES)
+    results = []
+    for k in range(count):
+        lower = turned[k - 1] if k > 0 else blank
+        upper = turned[k + 1] if k + 1 < count else blank
+        wrapped = jnp.where(source < 0, lower, upper)
+        results.append(jnp.where(inside, turned[k], wrapped))
+    return results
+
+
+def flow_kernel(
+    center_ref, other_ref, forward_ref, ahead_ref, center, other, turned, spill, score_f, score_b, top_f, top_b
+):
+    channels, padded_rows, breadth = center_ref.shape
+    parts = breadth // LANES
+    height = padded_rows - 2 * EDGE
+    other_rows = other_ref.shape[1]
+    lane = lax.broadcasted_iota(jnp.int32, (8, LANES), 1)
+    factor = score_scale * math.log2(math.e)
+
+    @pl.loop(0, channels)
+    def _(c):
+        for k in range(parts):
+            cols = slice(k * LANES, (k + 1) * LANES)
+            center[c, k] = center_ref[c, :, cols].astype(jnp.float32) * factor
+            other[c, k] = other_ref[c, :, cols].astype(jnp.float32)
+
+    top_f[...] = jnp.full(top_f.shape, -jnp.inf, jnp.float32)
+    top_b[...] = jnp.full(top_b.shape, -jnp.inf, jnp.float32)
+
+    @pl.loop(0, SPAN)
+    def _(col):
+        shift = col - RADIUS
+        long_lane = lax.broadcasted_iota(jnp.int32, (other_rows, LANES), 1)
+
+        @pl.loop(0, channels)
+        def _(c):
+            moved = shifted([other[c, k] for k in range(parts)], -shift, long_lane)
+            for k in range(parts):
+                turned[c, k] = moved[k]
+
+        @pl.loop(0, padded_rows // 16)
+        def _(pair):
+            base = pl.multiple_of(pair * 16, 16)
+            for k in range(parts):
+                sums = [[None] * SPAN for _ in range(2)]
+                for c in range(channels):
+                    mine = [center[c, k, pl.ds(base + 8 * j, 8), :] for j in range(2)]
+                    for offset in range(SPAN + 8):
+                        window = turned[c, k, pl.ds(base + EDGE - RADIUS + offset, 8), :]
+                        for j in range(2):
+                            row = offset - 8 * j
+                            if 0 <= row < SPAN:
+                                term = mine[j] * window
+                                sums[j][row] = term if c == 0 else sums[j][row] + term
+                for j in range(2):
+                    for row in range(SPAN):
+                        spill[row, k, pl.ds(base + 8 * j, 8), :] = sums[j][row]
+
+        @pl.loop(0, height // 8)
+        def _(block):
+            base = pl.multiple_of(block * 8, 8)
+            here = pl.ds(base, 8)
+            best_f = [top_f[k, here, :] for k in range(parts)]
+            best_b = [top_b[k, here, :] for k in range(parts)]
+            for row in range(SPAN):
+                for k in range(parts):
+                    value = spill[row, k, pl.ds(base + EDGE, 8), :]
+                    score_f[col, row, k, here, :] = value
+                    best_f[k] = jnp.maximum(best_f[k], value)
+                back = shifted(
+                    [spill[row, k, pl.ds(base + EDGE + RADIUS - row, 8), :] for k in range(parts)],
+                    shift,
+                    lane,
                 )
-            )
-    return score_scale * jnp.stack(scores)
-
-
-def flow_of(center, other):
-    channels, height, breadth = center.shape
-    band_rows = math.gcd(height, 16)
-
-    def one_band(band_index):
-        band_start = band_index * band_rows
-        center_band = lax.dynamic_slice_in_dim(center, band_start, band_rows, 1).astype(jnp.float32)
-        window_band = lax.dynamic_slice_in_dim(other, band_start, band_rows + 2 * RADIUS, 1).astype(
-            jnp.float32
-        )
-        return expected(band_scores(center_band, window_band, band_rows, breadth))
-
-    results = lax.map(one_band, jnp.arange(height // band_rows, dtype=jnp.int32))
-    return jnp.moveaxis(results, 0, 1).reshape(2, height, breadth)
+                for k in range(parts):
+                    score_b[col, row, k, here, :] = back[k]
+                    best_b[k] = jnp.maximum(best_b[k], back[k])
+            for k in range(parts):
+                top_f[k, here, :] = best_f[k]
+                top_b[k, here, :] = best_b[k]
+
+    for score, top, out_ref, sign in (
+        (score_f, top_f, forward_ref, 1.0),
+        (score_b, top_b, ahead_ref, -1.0),
+    ):
+
+        @pl.loop(0, height // 8)
+        def _(block):
+            here = pl.ds(pl.multiple_of(block * 8, 8), 8)
+            for k in range(parts):
+                best = top[k, here, :]
+
+                def one_column(col, carry):
+                    total, along_rows, along_cols = carry
+                    weights = [jnp.exp2(score[col, row, k, here, :] - best) for row in range(SPAN)]
+                    summed = weights[RADIUS]
+                    lean = None
+                    for step in range(1, RADIUS + 1):
+                        up, down = weights[RADIUS + step], weights[RADIUS - step]
+                        summed = summed + (up + down)
+                        part = (up - down) * float(step)
+                        lean = part if lean is None else lean + part
+                    place = (col - RADIUS).astype(jnp.float32)
+                    return total + summed, along_rows + lean, along_cols + summed * place
+
+                zero = jnp.zeros((8, LANES), jnp.float32)
+                total, along_rows, along_cols = lax.fori_loop(
+                    0, SPAN, one_column, (zero, zero, zero)
+                )
+                cols = slice(k * LANES, (k + 1) * LANES)
+                out_ref[0, here, cols] = sign * along_rows / total
+                out_ref[1, here, cols] = sign * along_cols / total
+
+
+def flows_between(center, other):
+    channels, padded_rows, breadth = center.shape
+    other_rows = other.shape[1]
+    parts = breadth // LANES
+    height = padded_rows - 2 * EDGE
+    shape = jax.ShapeDtypeStruct((2, height, breadth), jnp.float32)
+    vmem = pl.BlockSpec(memory_space=pltpu.VMEM)
+    return pl.pallas_call(
+        flow_kernel,
+        out_shape=(shape, shape),
+        in_specs=[vmem, vmem],
+        out_specs=(vmem, vmem),
+        scratch_shapes=[
+            pltpu.VMEM((channels, parts, padded_rows, LANES), jnp.float32),
+            pltpu.VMEM((channels, parts, other_rows, LANES), jnp.float32),
+            pltpu.VMEM((channels, parts, other_rows, LANES), jnp.float32),
+            pltpu.VMEM((SPAN, parts, padded_rows, LANES), jnp.float32),
+            pltpu.VMEM((SPAN, SPAN, parts, height, LANES), jnp.float32),
+            pltpu.VMEM((SPAN, SPAN, parts, height, LANES), jnp.float32),
+            pltpu.VMEM((parts, height, LANES), jnp.float32),
+            pltpu.VMEM((parts, height, LANES), jnp.float32),
+        ],
+        compiler_params=pltpu.CompilerParams(vmem_limit_bytes=48 * 1024 * 1024),
+    )(center, other)
+
+
+def sent(value, up, along):
+    axes = ("gz", "xy", "col")
+    sections = lax.axis_size("gz")
+    tiles = lax.axis_size(("xy", "col"))
+    pairs = [
+        (z * tiles + t, (z + up) * tiles + t + along)
+        for z in range(sections)
+        for t in range(tiles)
+        if 0 <= z + up < sections and 0 <= t + along < tiles
+    ]
+    return lax.ppermute(value, axes, pairs)
+
+
+def margins(middle, before, after, edge):
+    channels, rows, breadth = middle.shape
+    blank = jnp.zeros((channels, edge - RADIUS, breadth), middle.dtype)
+    return jnp.concatenate([blank, before, middle, after, blank], axis=1)
 
 
 def widen(values_in, margin):
@@ -127,10 +241,6 @@
     )
 
 
-def add_pair(earlier, later):
-    return earlier + later
-
-
 def on_device(features, class_map, stiffness, valid):
     center = features[0]
     height, breadth = (center.shape[1], center.shape[2])
@@ -144,16 +254,16 @@
         lax.dynamic_index_in_dim(link_all, jnp.maximum(section - 1, 0), 0, keepdims=False),
         0.0,
     )
-    padded = widen(padded_2(center, ((("xy", "col"), 1),), RADIUS), RADIUS)
-    upper_pad = passed_along(padded, "gz", -1)
-    forward = flow_of(center, upper_pad)
-    ahead_flow = flow_of(upper_pad[:, RADIUS : RADIUS + height, RADIUS : RADIUS + breadth], padded)
+    head, tail = (center[:, :RADIUS], center[:, height - RADIUS :])
+    other = margins(sent(center, -1, 0), sent(tail, -1, 1), sent(head, -1, -1), 2 * EDGE)
+    padded = margins(center, sent(tail, 0, 1), sent(head, 0, -1), EDGE)
+    forward, ahead_flow = flows_between(padded, other)
     passed = passed_along(jnp.stack([forward, ahead_flow]), "gz", 1)
     prior_flow = passed[0]
     backward = passed[1]
-    excess = link_here * forward - link_below * backward
-    before = entering(excess, "gz", add_pair, jnp.zeros_like(excess))
-    displace = 0.5 * (before - link_below * backward)
+    gathered = lax.all_gather(link_here * (forward - ahead_flow), "gz")
+    earlier = (jnp.arange(gathered.shape[0]) < section)[:, None, None, None]
+    displace = 0.5 * jnp.sum(jnp.where(earlier, gathered, 0.0), axis=0)
     levels = jnp.arange(stiffness.shape[0], dtype=jnp.int32)
     stiff_field = jnp.sum(
         jnp.where(class_map[0][None] == levels[:, None, None], stiffness[:, None, None], 0.0),

time: 263 us -> 163 us (0.62)
  other arithmetic: 136 us -> 8.24 us
  Pallas kernels: 0 us -> 69.2 us
  loops' own time: 18 us -> 0 us
  waiting for transfers between devices: 24.4 us -> 10.6 us
  local copies, waits for them, and re-layouts: 14.9 us -> 2.52 us
  starting transfers between devices: 52.8 us -> 55.9 us
    reduce_sum x88 -> x1, other arithmetic: 125 us -> 0.1 us  [on_device(): displace = 0.5 * jnp.sum(jnp.where(earlier, gathered, 0.0), axis=0)]
    pallas_call x0 -> x1, Pallas kernels: none -> 69.2 us  [flows_between(): pl.pallas_call(flow_kernel, out_shape=(shape, shape), in_specs=[vmem, vme...]
    another operation x3 -> x0, loops' own time: 18 us -> none  [the longest x2 17.9 us: flow_of(): lax.map(one_band, jnp.arange(height // band_rows, dtype=jnp.int32))]
    ppermute x8 -> x7, waiting for transfers between devices: 23.2 us -> 6.43 us  [passed_along(): lax.ppermute(value, axis, [(source, source + steps) for source in range(i...]
    ppermute x0 -> x5, starting transfers between devices: none -> 11.9 us  [sent(): return lax.ppermute(value, axes, pairs)]
    ppermute x5 -> x4, starting transfers between devices: 18.1 us -> 8.06 us  [padded_2(): lax.ppermute(head, axis, [((i + 1) % count, i) for i in range(ends)])]
    dynamic_slice x21 -> x1, local copies, waits for them, and re-layouts: 6.4 us -> 0.67 us  [on_device(): lax.dynamic_index_in_dim(link_all, jnp.maximum(section - 1, 0), 0, keepdi...]
    while x1352 -> x0, local copies, waits for them, and re-layouts: 4.97 us -> none
  transfers between devices with their start and end apart: 18 -> 20, of which waited for: 6 -> 6; matrix products, arithmetic and copies ran while one was open for 55% -> 3% of each run, Pallas kernels for 0% -> 0%
where the time goes in v1:
time: 163 us; the launch traced here: 162 us
  Pallas kernels  69.2 us (42%)
  starting transfers between devices  55.9 us (34%)
  blocking collectives  13.6 us (8%)
  waiting for transfers between devices  10.6 us (7%)
  other arithmetic  8.24 us (5%)
  local copies, waits for them, and re-layouts  2.52 us (2%)
  between operations  1.77 us (1%)
    pallas_call x1, Pallas kernels, flows_between(): pl.pallas_call(flow_kernel, out_shape=(shape, shape), in_specs=[vmem, vme...  69.2 us
    ppermute x7, starting transfers between devices, passed_along(): lax.ppermute(value, axis, [(source, source + steps) for source in range(i...  19 us
    ppermute x4, starting transfers between devices, padded_2(): lax.ppermute(tail, axis, [(i, (i + 1) % count) for i in range(ends)])  16.8 us
    all_gather x1, blocking collectives, on_device(): gathered = lax.all_gather(link_here * (forward - ahead_flow), 'gz')  13.6 us
    ppermute x5, starting transfers between devices, sent(): return lax.ppermute(value, axes, pairs)  11.9 us
    ppermute x4, starting transfers between devices, padded_2(): lax.ppermute(head, axis, [((i + 1) % count, i) for i in range(ends)])  8.06 us
    ppermute x7, waiting for transfers between devices, passed_along(): lax.ppermute(value, axis, [(source, source + steps) for source in range(i...  6.43 us
    ppermute x5, waiting for transfers between devices, sent(): return lax.ppermute(value, axes, pairs)  3.55 us
  transfers between devices with their start and end apart: 20, of which 6 were waited for; matrix products, arithmetic and copies ran while one was open for 3% of the time, Pallas kernels for 0%

profile of v1, /device:TPU:9, one launch (start us, length us, event | category | flops | bytes accessed | tf_op | source)
XLA Modules:
  0.0 161.7 jit_solution(5193984570194840356)
XLA Ops:
  0.6 2.1 %collective-permute-start.3 = (bf16[16,64,256]{2,1,0:T(8,128)(2,1)}, bf16[16,64,256]{2,1,0:T(8,128)(2,1)S(1)}, u32[]{:S(2)}, u32[]{:S(2)}) collective-permute-start(bf16[16,64,256]{2,1,0:T(8,128)(2,1)} %bitcast.57), channel_id=1, source_target_pairs={{4,0},{5,1},{6,2},{7,3},{8,4},{9,5},{10,6},{11,7},{12,8},{13,9},{1... | collective-permute-start | bytes 1572872 | tf_op jit(solution)/shard_map/ppermute | solution.py:207
  2.7 0.9 fusion.72
  3.6 2.9 %collective-permute-start.2 = (bf16[16,6,256]{2,1,0:T(8,128)(2,1)S(1)}, bf16[16,6,256]{2,1,0:T(8,128)(2,1)S(1)}, u32[]{:S(2)}, u32[]{:S(2)}) collective-permute-start(bf16[16,6,256]{2,1,0:T(8,128)(2,1)S(1)} %get-tuple-element.31), channel_id=1, source_target_pairs={{4,1},{5,2},{6,3},{8,5},{9,6},{10,7},{12,9},{13,10},{14,11},{20,17... | collective-permute-start | bytes 147464 | tf_op jit(solution)/shard_map/ppermute | solution.py:207
  6.5 3.1 %collective-permute-start = (bf16[16,6,256]{2,1,0:T(8,128)(2,1)S(1)}, bf16[16,6,256]{2,1,0:T(8,128)(2,1)S(1)}, u32[]{:S(2)}, u32[]{:S(2)}) collective-permute-start(bf16[16,6,256]{2,1,0:T(8,128)(2,1)S(1)} %get-tuple-element.31), channel_id=1, source_target_pairs={{0,1},{1,2},{2,3},{4,5},{5,6},{6,7},{8,9},{9,10},{10,11},{12,13},{... | collective-permute-start | bytes 147464 | tf_op jit(solution)/shard_map/ppermute | solution.py:207
  9.7 1.0 select_reduce_fusion.1
  10.6 1.9 %collective-permute-start.5 = (f32[1,256]{1,0:T(1,128)S(1)}, f32[1,256]{1,0:T(1,128)S(1)}, u32[]{:S(2)}, u32[]{:S(2)}) collective-permute-start(f32[1,256]{1,0:T(1,128)S(1)} %get-tuple-element.44), channel_id=1, source_target_pairs={{1,0},{2,1},{3,2},{5,4},{6,5},{7,6},{9,8},{10,9},{11,10},{13,12},{... | collective-permute-start | bytes 3080 | tf_op jit(solution)/shard_map/ppermute | solution.py:29
  12.6 3.6 %collective-permute-start.7 = (f32[1,256]{1,0:T(1,128)S(1)}, f32[1,256]{1,0:T(1,128)S(1)}, u32[]{:S(2)}, u32[]{:S(2)}) collective-permute-start(f32[1,256]{1,0:T(1,128)S(1)} %get-tuple-element.43), channel_id=1, source_target_pairs={{0,1},{1,2},{2,3},{4,5},{5,6},{6,7},{8,9},{9,10},{10,11},{12,13},{... | collective-permute-start | bytes 3080 | tf_op jit(solution)/shard_map/ppermute | solution.py:27
  16.2 0.9 fusion.71
  17.1 0.1 slice_reduce_fusion
  17.2 0.1 maximum_multiply_fusion
  17.3 0.7 fusion.77
  18.6 0.0 collective-permute-done.5
  18.6 1.9 %collective-permute-start.4 = (bf16[16,6,256]{2,1,0:T(8,128)(2,1)S(1)}, bf16[16,6,256]{2,1,0:T(8,128)(2,1)S(1)}, u32[]{:S(2)}, u32[]{:S(2)}) collective-permute-start(bf16[16,6,256]{2,1,0:T(8,128)(2,1)S(1)} %get-tuple-element.30), channel_id=1, source_target_pairs={{5,0},{6,1},{7,2},{9,4},{10,5},{11,6},{13,8},{14,9},{15,10},{21,16... | collective-permute-start | bytes 147464 | tf_op jit(solution)/shard_map/ppermute | solution.py:207
  20.6 0.0 collective-permute-done.7
  20.6 1.9 %collective-permute-start.1 = (bf16[16,6,256]{2,1,0:T(8,128)(2,1)S(1)}, bf16[16,6,256]{2,1,0:T(8,128)(2,1)S(1)}, u32[]{:S(2)}, u32[]{:S(2)}) collective-permute-start(bf16[16,6,256]{2,1,0:T(8,128)(2,1)S(1)} %get-tuple-element.30), channel_id=1, source_target_pairs={{1,0},{2,1},{3,2},{5,4},{6,5},{7,6},{9,8},{10,9},{11,10},{13,12},{... | collective-permute-start | bytes 147464 | tf_op jit(solution)/shard_map/ppermute | solution.py:207
  22.5 0.1 select_maximum_fusion.6
  22.6 0.0 collective-permute-done
  22.6 3.5 %collective-permute-done.1 = bf16[16,6,256]{2,1,0:T(8,128)(2,1)S(1)} collective-permute-done((bf16[16,6,256]{2,1,0:T(8,128)(2,1)S(1)}, bf16[16,6,256]{2,1,0:T(8,128)(2,1)S(1)}, u32[]{:S(2)}, u32[]{:S(2)}) %collective-permute-start.1) | collective-permute-done | bytes 49184 | tf_op jit(solution)/shard_map/ppermute | solution.py:207
  26.2 0.2 concatenate.46.center_ref
  26.4 0.0 collective-permute-done.2
  26.4 0.0 collective-permute-done.4
  26.4 0.0 collective-permute-done.3
  26.5 0.5 concatenate.47.other_ref
  27.0 69.2 %shard_map.59 = (f32[2,64,256]{2,1,0:T(8,128)}, f32[2,64,256]{2,1,0:T(8,128)S(1)}) custom-call(bf16[16,80,256]{2,1,0:T(8,128)(2,1)S(1)} %concatenate.46.center_ref, bf16[16,96,256]{2,1,0:T(8,128)(2,1)S(1)} %concatenate.47.other_ref), custom_call_target="tpu_custom_call" | custom-call | tf_op jit(solution)/shard_map/pallas_call | solution.py:178
  96.2 1.6 subtract_multiply_fusion
  97.8 0.0 copy-start
  97.8 13.6 %all-gather = f32[8,64,256]{2,1,0:T(8,128)S(1)} all-gather(f32[2,64,256]{2,1,0:T(8,128)S(1)} %subtract_multiply_fusion), channel_id=2, replica_groups=mesh['groups'=2,'gz'=4,'xy'=2,'col'=2] {'gz'}, dimensions={0}, use_global_device_ids=true | all-gather | bytes 655360 | tf_op jit(solution)/shard_map/all_gather | solution.py:264
  111.4 2.2 %collective-permute-start.11 = (f32[2,2,64,256]{3,2,1,0:T(8,128)S(1)}, f32[2,2,64,256]{3,2,1,0:T(8,128)S(1)}, u32[]{:S(2)}, u32[]{:S(2)}) collective-permute-start(f32[2,2,64,256]{3,2,1,0:T(8,128)S(1)} %pad_maximum_fusion), channel_id=1, source_target_pairs={{0,4},{4,8},{8,12},{1,5},{5,9},{9,13},{2,6},{6,10},{10,14},{3,7},{... | collective-permute-start | bytes 786440 | tf_op jit(solution)/shard_map/ppermute | solution.py:39
  113.6 0.1 select_reduce_fusion
  113.7 4.2 %collective-permute-start.10 = (bf16[2,64,256]{2,1,0:T(8,128)(2,1)S(1)}, bf16[2,64,256]{2,1,0:T(8,128)(2,1)S(1)}, u32[]{:S(2)}, u32[]{:S(2)}) collective-permute-start(bf16[2,64,256]{2,1,0:T(8,128)(2,1)S(1)} %fusion.66), channel_id=1, source_target_pairs={{0,4},{4,8},{8,12},{1,5},{5,9},{9,13},{2,6},{6,10},{10,14},{3,7},{... | collective-permute-start | bytes 196616 | tf_op jit(solution)/shard_map/ppermute | solution.py:39
  117.9 1.9 %collective-permute-start.9 = (bf16[2,64,256]{2,1,0:T(8,128)(2,1)S(1)}, bf16[2,64,256]{2,1,0:T(8,128)(2,1)S(1)}, u32[]{:S(2)}, u32[]{:S(2)}) collective-permute-start(bf16[2,64,256]{2,1,0:T(8,128)(2,1)S(1)} %fusion.66), channel_id=1, source_target_pairs={{4,0},{8,4},{12,8},{5,1},{9,5},{13,9},{6,2},{10,6},{14,10},{7,3},{... | collective-permute-start | bytes 196616 | tf_op jit(solution)/shard_map/ppermute | solution.py:39
  119.8 0.1 fusion.61
  119.9 2.1 %collective-permute-done.10 = bf16[2,64,256]{2,1,0:T(8,128)(2,1)S(1)} collective-permute-done((bf16[2,64,256]{2,1,0:T(8,128)(2,1)S(1)}, bf16[2,64,256]{2,1,0:T(8,128)(2,1)S(1)}, u32[]{:S(2)}, u32[]{:S(2)}) %collective-permute-start.10) | collective-permute-done | bytes 65568 | tf_op jit(solution)/shard_map/ppermute | solution.py:39
  122.0 1.6 collective-permute-done.9
  123.6 0.0 collective-permute-done.11
  123.6 0.1 multiply_reduce_fusion.11
  123.7 2.3 %collective-permute-start.6 = (f32[2,1,256]{2,1,0:T(1,128)S(1)}, f32[2,1,256]{2,1,0:T(1,128)S(1)}, u32[]{:S(2)}, u32[]{:S(2)}) collective-permute-start(f32[2,1,256]{2,1,0:T(1,128)S(1)} %get-tuple-element.39), channel_id=1, source_target_pairs={{1,0},{2,1},{3,2},{5,4},{6,5},{7,6},{9,8},{10,9},{11,10},{13,12},{... | collective-permute-start | bytes 6152 | tf_op jit(solution)/shard_map/ppermute | solution.py:29
  126.0 5.4 %collective-permute-start.8 = (f32[2,1,256]{2,1,0:T(1,128)S(1)}, f32[2,1,256]{2,1,0:T(1,128)S(1)}, u32[]{:S(2)}, u32[]{:S(2)}) collective-permute-start(f32[2,1,256]{2,1,0:T(1,128)S(1)} %get-tuple-element.38), channel_id=1, source_target_pairs={{0,1},{1,2},{2,3},{4,5},{5,6},{6,7},{8,9},{9,10},{10,11},{12,13},{... | collective-permute-start | bytes 6152 | tf_op jit(solution)/shard_map/ppermute | solution.py:27
  131.5 0.0 collective-permute-done.6
  131.5 0.6 collective-permute-done.8
  132.1 0.1 select_maximum_fusion.4
  132.3 0.9 fusion.69
  133.2 1.9 %collective-permute-start.12 = (f32[2,1,256]{2,1,0:T(1,128)S(1)}, f32[2,1,256]{2,1,0:T(1,128)S(1)}, u32[]{:S(2)}, u32[]{:S(2)}) collective-permute-start(f32[2,1,256]{2,1,0:T(1,128)S(1)} %get-tuple-element.37), channel_id=1, source_target_pairs={{1,0},{2,1},{3,2},{5,4},{6,5},{7,6},{9,8},{10,9},{11,10},{13,12},{... | collective-permute-start | bytes 6152 | tf_op jit(solution)/shard_map/ppermute | solution.py:29
  135.1 4.2 %collective-permute-start.13 = (f32[2,1,256]{2,1,0:T(1,128)S(1)}, f32[2,1,256]{2,1,0:T(1,128)S(1)}, u32[]{:S(2)}, u32[]{:S(2)}) collective-permute-start(f32[2,1,256]{2,1,0:T(1,128)S(1)} %get-tuple-element.36), channel_id=1, source_target_pairs={{0,1},{1,2},{2,3},{4,5},{5,6},{6,7},{8,9},{9,10},{10,11},{12,13},{... | collective-permute-start | bytes 6152 | tf_op jit(solution)/shard_map/ppermute | solution.py:27
  139.3 1.9 %collective-permute-start.14 = (bf16[2,64,256]{2,1,0:T(8,128)(2,1)S(1)}, bf16[2,64,256]{2,1,0:T(8,128)(2,1)S(1)}, u32[]{:S(2)}, u32[]{:S(2)}) collective-permute-start(bf16[2,64,256]{2,1,0:T(8,128)(2,1)S(1)} %get-tuple-element.26), channel_id=1, source_target_pairs={{4,0},{8,4},{12,8},{5,1},{9,5},{13,9},{6,2},{10,6},{14,10},{7,3},{... | collective-permute-start | bytes 196616 | tf_op jit(solution)/shard_map/ppermute | solution.py:39
  141.2 3.4 %collective-permute-start.15 = (bf16[2,64,256]{2,1,0:T(8,128)(2,1)S(1)}, bf16[2,64,256]{2,1,0:T(8,128)(2,1)S(1)}, u32[]{:S(2)}, u32[]{:S(2)}) collective-permute-start(bf16[2,64,256]{2,1,0:T(8,128)(2,1)S(1)} %get-tuple-element.26), channel_id=1, source_target_pairs={{0,4},{4,8},{8,12},{1,5},{5,9},{9,13},{2,6},{6,10},{10,14},{3,7},{... | collective-permute-start | bytes 196616 | tf_op jit(solution)/shard_map/ppermute | solution.py:39
  144.6 0.0 collective-permute-done.12
  144.6 0.0 collective-permute-done.13
  144.6 0.1 select_maximum_fusion.2
  144.8 0.0 collective-permute-done.14
  144.8 1.5 collective-permute-done.15
  146.3 0.1 multiply_reduce_fusion.7
  146.5 0.9 fusion.67
  147.4 1.9 %collective-permute-start.16 = (f32[2,1,256]{2,1,0:T(1,128)S(1)}, f32[2,1,256]{2,1,0:T(1,128)S(1)}, u32[]{:S(2)}, u32[]{:S(2)}) collective-permute-start(f32[2,1,256]{2,1,0:T(1,128)S(1)} %get-tuple-element.35), channel_id=1, source_target_pairs={{1,0},{2,1},{3,2},{5,4},{6,5},{7,6},{9,8},{10,9},{11,10},{13,12},{... | collective-permute-start | bytes 6152 | tf_op jit(solution)/shard_map/ppermute | solution.py:29
  149.4 3.6 %collective-permute-start.17 = (f32[2,1,256]{2,1,0:T(1,128)S(1)}, f32[2,1,256]{2,1,0:T(1,128)S(1)}, u32[]{:S(2)}, u32[]{:S(2)}) collective-permute-start(f32[2,1,256]{2,1,0:T(1,128)S(1)} %get-tuple-element.34), channel_id=1, source_target_pairs={{0,1},{1,2},{2,3},{4,5},{5,6},{6,7},{8,9},{9,10},{10,11},{12,13},{... | collective-permute-start | bytes 6152 | tf_op jit(solution)/shard_map/ppermute | solution.py:27
  153.0 1.9 %collective-permute-start.18 = (bf16[2,64,256]{2,1,0:T(8,128)(2,1)S(1)}, bf16[2,64,256]{2,1,0:T(8,128)(2,1)S(1)}, u32[]{:S(2)}, u32[]{:S(2)}) collective-permute-start(bf16[2,64,256]{2,1,0:T(8,128)(2,1)S(1)} %get-tuple-element.24), channel_id=1, source_target_pairs={{4,0},{8,4},{12,8},{5,1},{9,5},{13,9},{6,2},{10,6},{14,10},{7,3},{... | collective-permute-start | bytes 196616 | tf_op jit(solution)/shard_map/ppermute | solution.py:39
  154.9 3.6 %collective-permute-start.19 = (bf16[2,64,256]{2,1,0:T(8,128)(2,1)S(1)}, bf16[2,64,256]{2,1,0:T(8,128)(2,1)S(1)}, u32[]{:S(2)}, u32[]{:S(2)}) collective-permute-start(bf16[2,64,256]{2,1,0:T(8,128)(2,1)S(1)} %get-tuple-element.24), channel_id=1, source_target_pairs={{0,4},{4,8},{8,12},{1,5},{5,9},{9,13},{2,6},{6,10},{10,14},{3,7},{... | collective-permute-start | bytes 196616 | tf_op jit(solution)/shard_map/ppermute | solution.py:39
  158.5 0.0 collective-permute-done.16
  158.5 0.0 collective-permute-done.17
  158.5 0.1 select_maximum_fusion
  158.7 0.0 collective-permute-done.18
  158.7 1.3 collective-permute-done.19
  159.9 0.1 multiply_reduce_fusion.3
  160.2 1.6 fusion.21
  (22 shorter events, 0.4 us)
Async XLA Ops:
  0.6 25.5 %copy-start.1 = (bf16[1,16,64,256]{3,2,1,0:T(8,128)(2,1)S(1)}, bf16[1,16,64,256]{3,2,1,0:T(8,128)(2,1)}, u32[]{:S(2)}) copy-start(bf16[1,16,64,256]{3,2,1,0:T(8,128)(2,1)} %param.4) | copy-start | bytes 1572868
  0.6 25.8 %collective-permute-start.3 = (bf16[16,64,256]{2,1,0:T(8,128)(2,1)}, bf16[16,64,256]{2,1,0:T(8,128)(2,1)S(1)}, u32[]{:S(2)}, u32[]{:S(2)}) collective-permute-start(bf16[16,64,256]{2,1,0:T(8,128)(2,1)} %bitcast.57), channel_id=1, source_target_pairs={{4,0},{5,1},{6,2},{7,3},{8,4},{9,5},{10,6},{11,7},{12,8},{13,9},{1... | collective-permute-start | bytes 1572872 | tf_op jit(solution)/shard_map/ppermute | solution.py:207
  3.6 22.8 %collective-permute-start.2 = (bf16[16,6,256]{2,1,0:T(8,128)(2,1)S(1)}, bf16[16,6,256]{2,1,0:T(8,128)(2,1)S(1)}, u32[]{:S(2)}, u32[]{:S(2)}) collective-permute-start(bf16[16,6,256]{2,1,0:T(8,128)(2,1)S(1)} %get-tuple-element.31), channel_id=1, source_target_pairs={{4,1},{5,2},{6,3},{8,5},{9,6},{10,7},{12,9},{13,10},{14,11},{20,17... | collective-permute-start | bytes 147464 | tf_op jit(solution)/shard_map/ppermute | solution.py:207
  6.5 16.1 %collective-permute-start = (bf16[16,6,256]{2,1,0:T(8,128)(2,1)S(1)}, bf16[16,6,256]{2,1,0:T(8,128)(2,1)S(1)}, u32[]{:S(2)}, u32[]{:S(2)}) collective-permute-start(bf16[16,6,256]{2,1,0:T(8,128)(2,1)S(1)} %get-tuple-element.31), channel_id=1, source_target_pairs={{0,1},{1,2},{2,3},{4,5},{5,6},{6,7},{8,9},{9,10},{10,11},{12,13},{... | collective-permute-start | bytes 147464 | tf_op jit(solution)/shard_map/ppermute | solution.py:207
  10.6 8.0 %collective-permute-start.5 = (f32[1,256]{1,0:T(1,128)S(1)}, f32[1,256]{1,0:T(1,128)S(1)}, u32[]{:S(2)}, u32[]{:S(2)}) collective-permute-start(f32[1,256]{1,0:T(1,128)S(1)} %get-tuple-element.44), channel_id=1, source_target_pairs={{1,0},{2,1},{3,2},{5,4},{6,5},{7,6},{9,8},{10,9},{11,10},{13,12},{... | collective-permute-start | bytes 3080 | tf_op jit(solution)/shard_map/ppermute | solution.py:29
  12.6 8.0 %collective-permute-start.7 = (f32[1,256]{1,0:T(1,128)S(1)}, f32[1,256]{1,0:T(1,128)S(1)}, u32[]{:S(2)}, u32[]{:S(2)}) collective-permute-start(f32[1,256]{1,0:T(1,128)S(1)} %get-tuple-element.43), channel_id=1, source_target_pairs={{0,1},{1,2},{2,3},{4,5},{5,6},{6,7},{8,9},{9,10},{10,11},{12,13},{... | collective-permute-start | bytes 3080 | tf_op jit(solution)/shard_map/ppermute | solution.py:27
  18.6 7.8 %collective-permute-start.4 = (bf16[16,6,256]{2,1,0:T(8,128)(2,1)S(1)}, bf16[16,6,256]{2,1,0:T(8,128)(2,1)S(1)}, u32[]{:S(2)}, u32[]{:S(2)}) collective-permute-start(bf16[16,6,256]{2,1,0:T(8,128)(2,1)S(1)} %get-tuple-element.30), channel_id=1, source_target_pairs={{5,0},{6,1},{7,2},{9,4},{10,5},{11,6},{13,8},{14,9},{15,10},{21,16... | collective-permute-start | bytes 147464 | tf_op jit(solution)/shard_map/ppermute | solution.py:207
  20.6 5.6 %collective-permute-start.1 = (bf16[16,6,256]{2,1,0:T(8,128)(2,1)S(1)}, bf16[16,6,256]{2,1,0:T(8,128)(2,1)S(1)}, u32[]{:S(2)}, u32[]{:S(2)}) collective-permute-start(bf16[16,6,256]{2,1,0:T(8,128)(2,1)S(1)} %get-tuple-element.30), channel_id=1, source_target_pairs={{1,0},{2,1},{3,2},{5,4},{6,5},{7,6},{9,8},{10,9},{11,10},{13,12},{... | collective-permute-start | bytes 147464 | tf_op jit(solution)/shard_map/ppermute | solution.py:207
  97.8 13.6 %copy-start = (f32[2,64,256]{2,1,0:T(8,128)S(1)}, f32[2,64,256]{2,1,0:T(8,128)}, u32[]{:S(2)}) copy-start(f32[2,64,256]{2,1,0:T(8,128)} %get-tuple-element.4) | copy-start | bytes 393220
  111.4 12.2 %collective-permute-start.11 = (f32[2,2,64,256]{3,2,1,0:T(8,128)S(1)}, f32[2,2,64,256]{3,2,1,0:T(8,128)S(1)}, u32[]{:S(2)}, u32[]{:S(2)}) collective-permute-start(f32[2,2,64,256]{3,2,1,0:T(8,128)S(1)} %pad_maximum_fusion), channel_id=1, source_target_pairs={{0,4},{4,8},{8,12},{1,5},{5,9},{9,13},{2,6},{6,10},{10,14},{3,7},{... | collective-permute-start | bytes 786440 | tf_op jit(solution)/shard_map/ppermute | solution.py:39
  113.7 8.3 %collective-permute-start.10 = (bf16[2,64,256]{2,1,0:T(8,128)(2,1)S(1)}, bf16[2,64,256]{2,1,0:T(8,128)(2,1)S(1)}, u32[]{:S(2)}, u32[]{:S(2)}) collective-permute-start(bf16[2,64,256]{2,1,0:T(8,128)(2,1)S(1)} %fusion.66), channel_id=1, source_target_pairs={{0,4},{4,8},{8,12},{1,5},{5,9},{9,13},{2,6},{6,10},{10,14},{3,7},{... | collective-permute-start | bytes 196616 | tf_op jit(solution)/shard_map/ppermute | solution.py:39
  117.9 5.7 %collective-permute-start.9 = (bf16[2,64,256]{2,1,0:T(8,128)(2,1)S(1)}, bf16[2,64,256]{2,1,0:T(8,128)(2,1)S(1)}, u32[]{:S(2)}, u32[]{:S(2)}) collective-permute-start(bf16[2,64,256]{2,1,0:T(8,128)(2,1)S(1)} %fusion.66), channel_id=1, source_target_pairs={{4,0},{8,4},{12,8},{5,1},{9,5},{13,9},{6,2},{10,6},{14,10},{7,3},{... | collective-permute-start | bytes 196616 | tf_op jit(solution)/shard_map/ppermute | solution.py:39
  123.7 7.8 %collective-permute-start.6 = (f32[2,1,256]{2,1,0:T(1,128)S(1)}, f32[2,1,256]{2,1,0:T(1,128)S(1)}, u32[]{:S(2)}, u32[]{:S(2)}) collective-permute-start(f32[2,1,256]{2,1,0:T(1,128)S(1)} %get-tuple-element.39), channel_id=1, source_target_pairs={{1,0},{2,1},{3,2},{5,4},{6,5},{7,6},{9,8},{10,9},{11,10},{13,12},{... | collective-permute-start | bytes 6152 | tf_op jit(solution)/shard_map/ppermute | solution.py:29
  126.0 6.1 %collective-permute-start.8 = (f32[2,1,256]{2,1,0:T(1,128)S(1)}, f32[2,1,256]{2,1,0:T(1,128)S(1)}, u32[]{:S(2)}, u32[]{:S(2)}) collective-permute-start(f32[2,1,256]{2,1,0:T(1,128)S(1)} %get-tuple-element.38), channel_id=1, source_target_pairs={{0,1},{1,2},{2,3},{4,5},{5,6},{6,7},{8,9},{9,10},{10,11},{12,13},{... | collective-permute-start | bytes 6152 | tf_op jit(solution)/shard_map/ppermute | solution.py:27
  133.2 11.4 %collective-permute-start.12 = (f32[2,1,256]{2,1,0:T(1,128)S(1)}, f32[2,1,256]{2,1,0:T(1,128)S(1)}, u32[]{:S(2)}, u32[]{:S(2)}) collective-permute-start(f32[2,1,256]{2,1,0:T(1,128)S(1)} %get-tuple-element.37), channel_id=1, source_target_pairs={{1,0},{2,1},{3,2},{5,4},{6,5},{7,6},{9,8},{10,9},{11,10},{13,12},{... | collective-permute-start | bytes 6152 | tf_op jit(solution)/shard_map/ppermute | solution.py:29
  135.1 9.5 %collective-permute-start.13 = (f32[2,1,256]{2,1,0:T(1,128)S(1)}, f32[2,1,256]{2,1,0:T(1,128)S(1)}, u32[]{:S(2)}, u32[]{:S(2)}) collective-permute-start(f32[2,1,256]{2,1,0:T(1,128)S(1)} %get-tuple-element.36), channel_id=1, source_target_pairs={{0,1},{1,2},{2,3},{4,5},{5,6},{6,7},{8,9},{9,10},{10,11},{12,13},{... | collective-permute-start | bytes 6152 | tf_op jit(solution)/shard_map/ppermute | solution.py:27
  139.3 5.5 %collective-permute-start.14 = (bf16[2,64,256]{2,1,0:T(8,128)(2,1)S(1)}, bf16[2,64,256]{2,1,0:T(8,128)(2,1)S(1)}, u32[]{:S(2)}, u32[]{:S(2)}) collective-permute-start(bf16[2,64,256]{2,1,0:T(8,128)(2,1)S(1)} %get-tuple-element.26), channel_id=1, source_target_pairs={{4,0},{8,4},{12,8},{5,1},{9,5},{13,9},{6,2},{10,6},{14,10},{7,3},{... | collective-permute-start | bytes 196616 | tf_op jit(solution)/shard_map/ppermute | solution.py:39
  141.2 5.0 %collective-permute-start.15 = (bf16[2,64,256]{2,1,0:T(8,128)(2,1)S(1)}, bf16[2,64,256]{2,1,0:T(8,128)(2,1)S(1)}, u32[]{:S(2)}, u32[]{:S(2)}) collective-permute-start(bf16[2,64,256]{2,1,0:T(8,128)(2,1)S(1)} %get-tuple-element.26), channel_id=1, source_target_pairs={{0,4},{4,8},{8,12},{1,5},{5,9},{9,13},{2,6},{6,10},{10,14},{3,7},{... | collective-permute-start | bytes 196616 | tf_op jit(solution)/shard_map/ppermute | solution.py:39
  147.4 11.1 %collective-permute-start.16 = (f32[2,1,256]{2,1,0:T(1,128)S(1)}, f32[2,1,256]{2,1,0:T(1,128)S(1)}, u32[]{:S(2)}, u32[]{:S(2)}) collective-permute-start(f32[2,1,256]{2,1,0:T(1,128)S(1)} %get-tuple-element.35), channel_id=1, source_target_pairs={{1,0},{2,1},{3,2},{5,4},{6,5},{7,6},{9,8},{10,9},{11,10},{13,12},{... | collective-permute-start | bytes 6152 | tf_op jit(solution)/shard_map/ppermute | solution.py:29
  149.4 9.2 %collective-permute-start.17 = (f32[2,1,256]{2,1,0:T(1,128)S(1)}, f32[2,1,256]{2,1,0:T(1,128)S(1)}, u32[]{:S(2)}, u32[]{:S(2)}) collective-permute-start(f32[2,1,256]{2,1,0:T(1,128)S(1)} %get-tuple-element.34), channel_id=1, source_target_pairs={{0,1},{1,2},{2,3},{4,5},{5,6},{6,7},{8,9},{9,10},{10,11},{12,13},{... | collective-permute-start | bytes 6152 | tf_op jit(solution)/shard_map/ppermute | solution.py:27
  153.0 5.7 %collective-permute-start.18 = (bf16[2,64,256]{2,1,0:T(8,128)(2,1)S(1)}, bf16[2,64,256]{2,1,0:T(8,128)(2,1)S(1)}, u32[]{:S(2)}, u32[]{:S(2)}) collective-permute-start(bf16[2,64,256]{2,1,0:T(8,128)(2,1)S(1)} %get-tuple-element.24), channel_id=1, source_target_pairs={{4,0},{8,4},{12,8},{5,1},{9,5},{13,9},{6,2},{10,6},{14,10},{7,3},{... | collective-permute-start | bytes 196616 | tf_op jit(solution)/shard_map/ppermute | solution.py:39
  154.9 5.0 %collective-permute-start.19 = (bf16[2,64,256]{2,1,0:T(8,128)(2,1)S(1)}, bf16[2,64,256]{2,1,0:T(8,128)(2,1)S(1)}, u32[]{:S(2)}, u32[]{:S(2)}) collective-permute-start(bf16[2,64,256]{2,1,0:T(8,128)(2,1)S(1)} %get-tuple-element.24), channel_id=1, source_target_pairs={{0,4},{4,8},{8,12},{1,5},{5,9},{9,13},{2,6},{6,10},{10,14},{3,7},{... | collective-permute-start | bytes 196616 | tf_op jit(solution)/shard_map/ppermute | solution.py:39

commit v2 on v1

--- a/solution.py
+++ b/solution.py
@@ -14,33 +14,6 @@
 score_scale = 0.25
 step_size = 0.1
 saturation = 2.0
-
-
-def padded_2(cells, sides, width):
-    for axis, dim in sides:
-        count = lax.axis_size(axis)
-        ends = count - 1
-        head = lax.slice_in_dim(cells, 0, width, axis=dim)
-        tail = lax.slice_in_dim(cells, cells.shape[dim] - width, cells.shape[dim], axis=dim)
-        cells = jnp.concatenate(
-            [
-                lax.ppermute(tail, axis, [(i, (i + 1) % count) for i in range(ends)]),
-                cells,
-                lax.ppermute(head, axis, [((i + 1) % count, i) for i in range(ends)]),
-            ],
-            axis=dim,
-        )
-    return cells
-
-
-def passed_along(value, axis, steps):
-    count = lax.axis_size(axis)
-    initial, last = (max(0, -steps), min(count, count - steps))
-    return lax.ppermute(value, axis, [(source, source + steps) for source in range(initial, last)])
-
-
-def shortened(shard):
-    return jax.tree.map(lambda a: a.astype(jnp.bfloat16) if a.dtype == jnp.float32 else a, shard)
 
 
 LANES = 128
@@ -213,32 +186,316 @@
     return jnp.concatenate([blank, before, middle, after, blank], axis=1)
 
 
-def widen(values_in, margin):
-    padding = [(0, 0)] * (values_in.ndim - 1) + [(margin, margin)]
-    return jnp.pad(values_in, padding)
-
-
-def elastic_term(disp_pad, stiff_pad):
-    middle = disp_pad[..., 1:-1, 1:-1]
-    stiff_mid = stiff_pad[..., 1:-1, 1:-1]
-    result = jnp.zeros_like(middle)
-    for row_part, col_part in (
-        (slice(2, None), slice(1, -1)),
-        (slice(0, -2), slice(1, -1)),
-        (slice(1, -1), slice(2, None)),
-        (slice(1, -1), slice(0, -2)),
-    ):
-        neighbour_stiff = stiff_pad[..., row_part, col_part]
-        result = result + 0.5 * (stiff_mid + neighbour_stiff) * (
-            middle - disp_pad[..., row_part, col_part]
+def spread(first, second):
+    return lax.rsqrt(1.0 + (first * first + second * second) / (saturation * saturation))
+
+
+def relax_kernel(
+    links_ref,
+    forward_ref,
+    ahead_ref,
+    stiff_ref,
+    out_ref,
+    stiff,
+    disp,
+    prior,
+    backward,
+    summed,
+    summed_in,
+    above,
+    below,
+    rounded,
+    above_in,
+    below_in,
+    flow_send,
+    flow_recv,
+    sum_send,
+    sum_recv,
+    stiff_send,
+    stiff_recv,
+    row_send,
+    row_recv,
+    sect_send,
+    sect_recv,
+):
+    height, breadth = stiff_ref.shape
+    sections = lax.axis_size("gz")
+    wide = lax.axis_size("col")
+    tiles = lax.axis_size("xy") * wide
+    section = lax.axis_index("gz")
+    tile = lax.axis_index("xy") * wide + lax.axis_index("col")
+    link_here = links_ref[0]
+    link_below = links_ref[1]
+
+    def tile_at(t):
+        return {"xy": t // wide, "col": lax.rem(t, wide)}
+
+    next_tile, prior_tile = tile_at(tile + 1), tile_at(tile + tiles - 1 - tiles * (tile > 0))
+    next_section, prior_section = {"gz": section + 1}, {"gz": section - 1}
+    has_next_tile, has_prior_tile = tile + 1 < tiles, tile > 0
+    has_next, has_prior = section + 1 < sections, section > 0
+    partners = (
+        (has_next_tile, next_tile),
+        (has_prior_tile, prior_tile),
+        (has_next, next_section),
+        (has_prior, prior_section),
+    )
+
+    top, bottom = slice(0, EDGE), slice(EDGE + height, 2 * EDGE + height)
+    first, last = slice(EDGE, 2 * EDGE), slice(height, EDGE + height)
+    for edge in (top, bottom):
+        stiff[edge, :] = jnp.zeros((EDGE, breadth), jnp.float32)
+        for step in range(STEPS):
+            for part in range(2):
+                disp[step, part, edge, :] = jnp.zeros((EDGE, breadth), jnp.float32)
+    for array in (prior, backward, summed_in):
+        array[...] = jnp.zeros(array.shape, array.dtype)
+    above_in[...] = jnp.zeros(above_in.shape, above_in.dtype)
+    below_in[...] = jnp.zeros(below_in.shape, below_in.dtype)
+    stiff[EDGE : EDGE + height, :] = stiff_ref[...]
+
+    barrier = pltpu.get_barrier_semaphore()
+    count = jnp.int32(0)
+    for present, partner in partners:
+        count = count + present.astype(jnp.int32)
+
+        @pl.when(present)
+        def _():
+            pl.semaphore_signal(
+                barrier, inc=1, device_id=partner, device_id_type=pl.DeviceIdType.MESH
+            )
+
+    pl.semaphore_wait(barrier, count)
+
+    pending = []
+
+    def send(condition, source, target, send_sem, recv_sem, partner):
+        copy = pltpu.make_async_remote_copy(
+            src_ref=source,
+            dst_ref=target,
+            send_sem=send_sem,
+            recv_sem=recv_sem,
+            device_id=partner,
+            device_id_type=pl.DeviceIdType.MESH,
         )
-    return result
-
-
-def spring(vector):
-    return vector / jnp.sqrt(
-        1.0 + jnp.sum(vector * vector, axis=-3, keepdims=True) / (saturation * saturation)
-    )
+
+        @pl.when(condition)
+        def _():
+            copy.start()
+
+        pending.append((condition, copy))
+        return copy
+
+    def arrive(condition, copy):
+        @pl.when(condition)
+        def _():
+            copy.wait_recv()
+
+    flows = []
+    for part in range(2):
+        pieces = []
+        for which, (source, target) in enumerate(((forward_ref, prior), (ahead_ref, backward))):
+            pieces.append(
+                send(
+                    has_next,
+                    source.at[part],
+                    target.at[part],
+                    flow_send.at[part, which],
+                    flow_recv.at[part, which],
+                    next_section,
+                )
+            )
+        flows.append(pieces)
+    stiff_down = send(
+        has_next_tile, stiff.at[last], stiff.at[top], stiff_send.at[0], stiff_recv.at[0], next_tile
+    )
+    stiff_up = send(
+        has_prior_tile, stiff.at[first], stiff.at[bottom], stiff_send.at[1], stiff_recv.at[1], prior_tile
+    )
+
+    def send_rows(step):
+        down = send(
+            has_next_tile,
+            disp.at[step, :, last],
+            disp.at[step, :, top],
+            row_send.at[step, 0],
+            row_recv.at[step, 0],
+            next_tile,
+        )
+        up = send(
+            has_prior_tile,
+            disp.at[step, :, first],
+            disp.at[step, :, bottom],
+            row_send.at[step, 1],
+            row_recv.at[step, 1],
+            prior_tile,
+        )
+        return down, up
+
+    for part in range(2):
+        for copy in flows[part]:
+            arrive(has_prior, copy)
+        chain = pltpu.make_async_remote_copy(
+            src_ref=summed.at[part],
+            dst_ref=summed_in.at[part],
+            send_sem=sum_send.at[part],
+            recv_sem=sum_recv.at[part],
+            device_id=next_section,
+            device_id_type=pl.DeviceIdType.MESH,
+        )
+        arrive(section > 1, chain)
+        before = summed_in[part]
+        here = before + link_below * (prior[part] - backward[part])
+        summed[part] = here
+        send(
+            has_next & has_prior,
+            summed.at[part],
+            summed_in.at[part],
+            sum_send.at[part],
+            sum_recv.at[part],
+            next_section,
+        )
+        disp[0, part, EDGE : EDGE + height, :] = 0.5 * here
+        below[part] = 0.5 * before
+        above[part] = 0.5 * (here + link_here * (forward_ref[part] - ahead_ref[part]))
+
+    rows = send_rows(0)
+    arrive(has_prior_tile, stiff_down)
+    arrive(has_next_tile, stiff_up)
+    lane = lax.broadcasted_iota(jnp.int32, (16, breadth), 1)
+    at_left, at_right = lane == 0, lane == breadth - 1
+
+    def left_of(value):
+        return jnp.where(at_left, 0.0, pltpu.roll(value, 1, 1))
+
+    def right_of(value):
+        return jnp.where(at_right, 0.0, pltpu.roll(value, breadth - 1, 1))
+
+    crossing = None
+    for step in range(STEPS):
+        arrive(has_prior_tile, rows[0])
+        arrive(has_next_tile, rows[1])
+        if crossing is not None:
+            arrive(has_next, crossing[0])
+            arrive(has_prior, crossing[1])
+
+        @pl.loop(0, height // 16)
+        def _(block):
+            base = pl.multiple_of(block * 16, 16)
+            here = pl.ds(base, 16)
+            inner = pl.ds(pl.multiple_of(base + EDGE, EDGE), 16)
+            around = pl.ds(base, 16 + 2 * EDGE)
+            stiff_all = stiff[around, :]
+            middle_stiff = stiff_all[EDGE : EDGE + 16]
+            weights = [
+                0.5 * (middle_stiff + neighbour)
+                for neighbour in (
+                    stiff_all[EDGE + 1 : EDGE + 17],
+                    stiff_all[EDGE - 1 : EDGE + 15],
+                    right_of(middle_stiff),
+                    left_of(middle_stiff),
+                )
+            ]
+            windows = [disp[step, part, around, :] for part in range(2)]
+            middles = [window[EDGE : EDGE + 16] for window in windows]
+            if step == 0:
+                uppers = [above[part, here, :] for part in range(2)]
+                lowers = [below[part, here, :] for part in range(2)]
+            else:
+                uppers = [above_in[step - 1, part, here, :].astype(jnp.float32) for part in range(2)]
+                lowers = [below_in[step - 1, part, here, :].astype(jnp.float32) for part in range(2)]
+            gradients = []
+            for part in range(2):
+                middle = middles[part]
+                neighbours = (
+                    windows[part][EDGE + 1 : EDGE + 17],
+                    windows[part][EDGE - 1 : EDGE + 15],
+                    right_of(middle),
+                    left_of(middle),
+                )
+                total = weights[0] * (middle - neighbours[0])
+                for k in range(1, 4):
+                    total = total + weights[k] * (middle - neighbours[k])
+                gradients.append(total)
+            for sign, link, others, flow in (
+                (-1.0, link_here, uppers, forward_ref),
+                (-1.0, link_below, lowers, backward),
+                (1.0, link_below, lowers, prior),
+                (1.0, link_here, uppers, ahead_ref),
+            ):
+                vector = [
+                    -sign * (others[part] - middles[part]) - flow[part, here, :] for part in range(2)
+                ]
+                scale = (sign * link) * spread(*vector)
+                for part in range(2):
+                    gradients[part] = gradients[part] + scale * vector[part]
+            for part in range(2):
+                updated = middles[part] - step_size * gradients[part]
+                if step == STEPS - 1:
+                    out_ref[part, here, :] = updated
+                else:
+                    disp[step + 1, part, inner, :] = updated
+                    rounded[step, part, here, :] = updated.astype(rounded.dtype)
+
+        if step < STEPS - 1:
+            crossing = (
+                send(
+                    has_prior,
+                    rounded.at[step],
+                    above_in.at[step],
+                    sect_send.at[step, 0],
+                    sect_recv.at[step, 0],
+                    prior_section,
+                ),
+                send(
+                    has_next,
+                    rounded.at[step],
+                    below_in.at[step],
+                    sect_send.at[step, 1],
+                    sect_recv.at[step, 1],
+                    next_section,
+                ),
+            )
+            rows = send_rows(step + 1)
+
+    for condition, copy in pending:
+
+        @pl.when(condition)
+        def _():
+            copy.wait_send()
+
+
+def relaxed(links, forward, ahead, stiff_field):
+    height, breadth = stiff_field.shape
+    vmem = pl.BlockSpec(memory_space=pltpu.VMEM)
+    pair = (2, height, breadth)
+    moved = (STEPS - 1, 2, height, breadth)
+    dma = pltpu.SemaphoreType.DMA
+    return pl.pallas_call(
+        relax_kernel,
+        out_shape=jax.ShapeDtypeStruct(pair, jnp.float32),
+        in_specs=[pl.BlockSpec(memory_space=pltpu.SMEM), vmem, vmem, vmem],
+        out_specs=vmem,
+        scratch_shapes=[
+            pltpu.VMEM((height + 2 * EDGE, breadth), jnp.float32),
+            pltpu.VMEM((STEPS, 2, height + 2 * EDGE, breadth), jnp.float32),
+            *[pltpu.VMEM(pair, jnp.float32) for _ in range(6)],
+            *[pltpu.VMEM(moved, jnp.bfloat16) for _ in range(3)],
+            dma((2, 2)),
+            dma((2, 2)),
+            dma((2,)),
+            dma((2,)),
+            dma((2,)),
+            dma((2,)),
+            dma((STEPS, 2)),
+            dma((STEPS, 2)),
+            dma((STEPS - 1, 2)),
+            dma((STEPS - 1, 2)),
+        ],
+        compiler_params=pltpu.CompilerParams(
+            collective_id=0, has_side_effects=True, vmem_limit_bytes=16 * 1024 * 1024
+        ),
+    )(links, forward, ahead, stiff_field)
 
 
 def on_device(features, class_map, stiffness, valid):
@@ -258,29 +515,12 @@
     other = margins(sent(center, -1, 0), sent(tail, -1, 1), sent(head, -1, -1), 2 * EDGE)
     padded = margins(center, sent(tail, 0, 1), sent(head, 0, -1), EDGE)
     forward, ahead_flow = flows_between(padded, other)
-    passed = passed_along(jnp.stack([forward, ahead_flow]), "gz", 1)
-    prior_flow = passed[0]
-    backward = passed[1]
-    gathered = lax.all_gather(link_here * (forward - ahead_flow), "gz")
-    earlier = (jnp.arange(gathered.shape[0]) < section)[:, None, None, None]
-    displace = 0.5 * jnp.sum(jnp.where(earlier, gathered, 0.0), axis=0)
     levels = jnp.arange(stiffness.shape[0], dtype=jnp.int32)
     stiff_field = jnp.sum(
         jnp.where(class_map[0][None] == levels[:, None, None], stiffness[:, None, None], 0.0),
         axis=0,
     )
-    stiff_pad = widen(padded_2(stiff_field, ((("xy", "col"), 0),), 1), 1)
-    for step_number in range(STEPS):
-        disp_pad = widen(padded_2(displace, ((("xy", "col"), 1),), 1), 1)
-        elastic = elastic_term(disp_pad, stiff_pad)
-        upper_disp = passed_along(shortened(displace), "gz", -1).astype(displace.dtype)
-        lower_disp = passed_along(shortened(displace), "gz", 1).astype(displace.dtype)
-        pull_up = link_here * spring(upper_disp - displace - forward)
-        pull_down = link_below * spring(lower_disp - displace - backward)
-        from_below = link_below * spring(displace - lower_disp - prior_flow)
-        from_above = link_here * spring(displace - upper_disp - ahead_flow)
-        gradient = elastic - pull_up - pull_down + from_below + from_above
-        displace = displace - step_size * gradient
+    displace = relaxed(jnp.stack([link_here, link_below]), forward, ahead_flow, stiff_field)
     return (displace[None], forward[None])
 
 

time: 163 us -> 116 us (0.71)
  starting transfers between devices: 55.9 us -> 11.9 us
  Pallas kernels: 69.2 us -> 94.4 us
  blocking collectives: 13.6 us -> 0 us
  waiting for transfers between devices: 10.6 us -> 0.83 us
  other arithmetic: 8.24 us -> 1.08 us
  local copies, waits for them, and re-layouts: 2.52 us -> 6.39 us
    ppermute x15 -> x0, starting transfers between devices: 43.9 us -> none  [the longest x7 19 us: passed_along(): lax.ppermute(value, axis, [(source, source + steps) for source in range(i...]
    pallas_call x0 -> x1, Pallas kernels: none -> 25.2 us  [relaxed(): pl.pallas_call(relax_kernel, out_shape=jax.ShapeDtypeStruct(pair, jnp.flo...]
    all_gather x1 -> x0, blocking collectives: 13.6 us -> none  [on_device(): gathered = lax.all_gather(link_here * (forward - ahead_flow), 'gz')]
    ppermute x15 -> x0, waiting for transfers between devices: 7.04 us -> none  [the longest x7 6.43 us: passed_along(): lax.ppermute(value, axis, [(source, source + steps) for source in range(i...]
    ppermute x5, waiting for transfers between devices: 3.55 us -> 0.83 us  [sent(): return lax.ppermute(value, axes, pairs)]
    unnamed x4 -> x9, local copies, waits for them, and re-layouts: 0.01 us -> 2.21 us
    convert_element_type x3 -> x0, other arithmetic: 1.86 us -> none  [shortened(): a.astype(jnp.bfloat16)]
    concatenate x2, local copies, waits for them, and re-layouts: 0.77 us -> 2.55 us  [margins(): return jnp.concatenate([blank, before, middle, after, blank], axis=1)]
  transfers between devices with their start and end apart: 20 -> 5, of which waited for: 6 -> 1; matrix products, arithmetic and copies ran while one was open for 3% -> 4% of each run, Pallas kernels for 0% -> 0%
where the time goes in v2:
time: 116 us
  Pallas kernels  94.4 us (81%)
  starting transfers between devices  11.9 us (10%)
  local copies, waits for them, and re-layouts  6.39 us (6%)
  between operations  1.44 us (1%)
    pallas_call x1, Pallas kernels, flows_between(): pl.pallas_call(flow_kernel, out_shape=(shape, shape), in_specs=[vmem, vme...  69.2 us
    pallas_call x1, Pallas kernels, relaxed(): pl.pallas_call(relax_kernel, out_shape=jax.ShapeDtypeStruct(pair, jnp.flo...  25.2 us
    ppermute x5, starting transfers between devices, sent(): return lax.ppermute(value, axes, pairs)  11.9 us
    concatenate x2, local copies, waits for them, and re-layouts, margins(): return jnp.concatenate([blank, before, middle, after, blank], axis=1)  2.55 us
  transfers between devices with their start and end apart: 5, of which 1 were waited for; matrix products, arithmetic and copies ran while one was open for 4% of the time, Pallas kernels for 0%

profile of v2, /device:TPU:9, one launch (start us, length us, event | category | flops | bytes accessed | tf_op | source)
XLA Modules:
  0.0 116.0 jit_solution(15893695745114501256)
XLA Ops:
  0.6 1.9 %collective-permute-start.3 = (bf16[16,64,256]{2,1,0:T(8,128)(2,1)}, bf16[16,64,256]{2,1,0:T(8,128)(2,1)S(1)}, u32[]{:S(2)}, u32[]{:S(2)}) collective-permute-start(bf16[16,64,256]{2,1,0:T(8,128)(2,1)} %bitcast.8), channel_id=1, source_target_pairs={{4,0},{5,1},{6,2},{7,3},{8,4},{9,5},{10,6},{11,7},{12,8},{13,9},{1... | collective-permute-start | bytes 1572872 | tf_op jit(solution)/shard_map/ppermute | solution.py:180
  2.6 0.0 copy-start.2
  2.6 0.9 fusion.1
  3.5 0.0 copy-start.1
  3.5 3.1 %collective-permute-start.2 = (bf16[16,6,256]{2,1,0:T(8,128)(2,1)S(1)}, bf16[16,6,256]{2,1,0:T(8,128)(2,1)S(1)}, u32[]{:S(2)}, u32[]{:S(2)}) collective-permute-start(bf16[16,6,256]{2,1,0:T(8,128)(2,1)S(1)} %get-tuple-element.9), channel_id=1, source_target_pairs={{4,1},{5,2},{6,3},{8,5},{9,6},{10,7},{12,9},{13,10},{14,11},{20,17... | collective-permute-start | bytes 147464 | tf_op jit(solution)/shard_map/ppermute | solution.py:180
  6.6 3.1 %collective-permute-start = (bf16[16,6,256]{2,1,0:T(8,128)(2,1)S(1)}, bf16[16,6,256]{2,1,0:T(8,128)(2,1)S(1)}, u32[]{:S(2)}, u32[]{:S(2)}) collective-permute-start(bf16[16,6,256]{2,1,0:T(8,128)(2,1)S(1)} %get-tuple-element.9), channel_id=1, source_target_pairs={{0,1},{1,2},{2,3},{4,5},{5,6},{6,7},{8,9},{9,10},{10,11},{12,13},{... | collective-permute-start | bytes 147464 | tf_op jit(solution)/shard_map/ppermute | solution.py:180
  9.7 1.9 %collective-permute-start.4 = (bf16[16,6,256]{2,1,0:T(8,128)(2,1)S(1)}, bf16[16,6,256]{2,1,0:T(8,128)(2,1)S(1)}, u32[]{:S(2)}, u32[]{:S(2)}) collective-permute-start(bf16[16,6,256]{2,1,0:T(8,128)(2,1)S(1)} %get-tuple-element.8), channel_id=1, source_target_pairs={{5,0},{6,1},{7,2},{9,4},{10,5},{11,6},{13,8},{14,9},{15,10},{21,16... | collective-permute-start | bytes 147464 | tf_op jit(solution)/shard_map/ppermute | solution.py:180
  11.6 1.9 %collective-permute-start.1 = (bf16[16,6,256]{2,1,0:T(8,128)(2,1)S(1)}, bf16[16,6,256]{2,1,0:T(8,128)(2,1)S(1)}, u32[]{:S(2)}, u32[]{:S(2)}) collective-permute-start(bf16[16,6,256]{2,1,0:T(8,128)(2,1)S(1)} %get-tuple-element.8), channel_id=1, source_target_pairs={{1,0},{2,1},{3,2},{5,4},{6,5},{7,6},{9,8},{10,9},{11,10},{13,12},{... | collective-permute-start | bytes 147464 | tf_op jit(solution)/shard_map/ppermute | solution.py:180
  13.5 0.0 copy-done.2
  13.5 0.2 fusion
  13.7 0.1 slice_reduce_fusion
  13.8 0.1 maximum_multiply_fusion
  13.9 0.6 fusion.2
  15.2 0.0 copy-start.3
  15.2 0.0 copy-done.1
  15.2 0.6 copy-done.3
  15.8 0.1 select_reduce_fusion.stiff_ref
  15.9 0.7 pad_maximum_fusion.links_ref
  16.7 0.0 collective-permute-done
  16.7 0.8 collective-permute-done.1
  17.5 2.0 %concatenate.10.center_ref = bf16[16,80,256]{2,1,0:T(8,128)(2,1)S(1)} concatenate(bf16[16,2,256]{2,1,0:T(2,128)(2,1)S(1)} %broadcast_in_dim.26, bf16[16,6,256]{2,1,0:T(8,128)(2,1)S(1)} %collective-permute-done, bf16[16,64,256]{2,1,0:T(8,128)(2,1)} %bitcast.10, bf16[16,6,256]{2,1,0:T(8,128)(2,1)S(1)} %collective-permute-done.1, bf16[16,2,256]{2,1,0:T(2,128)(2,1)S(1)} %broadcast_in_dim.26), dimensions={1} | concatenate | bytes 1310720 | tf_op jit(solution)/shard_map/concatenate | solution.py:186
  19.5 0.0 collective-permute-done.2
  19.5 0.0 collective-permute-done.4
  19.5 0.0 collective-permute-done.3
  19.6 0.5 concatenate.11.other_ref
  20.1 69.2 %shard_map.59 = (f32[2,64,256]{2,1,0:T(8,128)}, f32[2,64,256]{2,1,0:T(8,128)S(1)}) custom-call(bf16[16,80,256]{2,1,0:T(8,128)(2,1)S(1)} %concatenate.10.center_ref, bf16[16,96,256]{2,1,0:T(8,128)(2,1)S(1)} %concatenate.11.other_ref), custom_call_target="tpu_custom_call" | custom-call | tf_op jit(solution)/shard_map/pallas_call | solution.py:151
  89.3 0.0 copy-start
  89.3 0.9 copy-done
  90.2 25.2 %shard_map.60 = f32[2,64,256]{2,1,0:T(8,128)S(1)} custom-call(f32[2]{0:T(128)S(1)} %pad_maximum_fusion.links_ref, f32[2,64,256]{2,1,0:T(8,128)S(1)} %copy-done, f32[2,64,256]{2,1,0:T(8,128)S(1)} %get-tuple-element.5.ahead_ref, f32[64,256]{1,0:T(8,128)S(1)} %select_reduce_fusion.stiff_ref), custom_call_target="tpu_custom_call" | custom-call | tf_op jit(solution)/shard_map/pallas_call | solution.py:474
  115.4 0.7 copy.7
  (2 shorter events, 0.0 us)
Async XLA Ops:
  0.6 18.9 %collective-permute-start.3 = (bf16[16,64,256]{2,1,0:T(8,128)(2,1)}, bf16[16,64,256]{2,1,0:T(8,128)(2,1)S(1)}, u32[]{:S(2)}, u32[]{:S(2)}) collective-permute-start(bf16[16,64,256]{2,1,0:T(8,128)(2,1)} %bitcast.8), channel_id=1, source_target_pairs={{4,0},{5,1},{6,2},{7,3},{8,4},{9,5},{10,6},{11,7},{12,8},{13,9},{1... | collective-permute-start | bytes 1572872 | tf_op jit(solution)/shard_map/ppermute | solution.py:180
  2.6 11.0 %copy-start.2 = (s32[4,4]{1,0:T(4,128)S(1)}, s32[4,4]{1,0:T(4,128)}, u32[]{:S(2)}) copy-start(s32[4,4]{1,0:T(4,128)} %param.7) | copy-start | bytes 196
  3.5 11.7 %copy-start.1 = (s32[1,64,256]{2,1,0:T(8,128)S(1)}, s32[1,64,256]{2,1,0:T(8,128)}, u32[]{:S(2)}) copy-start(s32[1,64,256]{2,1,0:T(8,128)} %param.5) | copy-start | bytes 196612
  3.5 16.0 %collective-permute-start.2 = (bf16[16,6,256]{2,1,0:T(8,128)(2,1)S(1)}, bf16[16,6,256]{2,1,0:T(8,128)(2,1)S(1)}, u32[]{:S(2)}, u32[]{:S(2)}) collective-permute-start(bf16[16,6,256]{2,1,0:T(8,128)(2,1)S(1)} %get-tuple-element.9), channel_id=1, source_target_pairs={{4,1},{5,2},{6,3},{8,5},{9,6},{10,7},{12,9},{13,10},{14,11},{20,17... | collective-permute-start | bytes 147464 | tf_op jit(solution)/shard_map/ppermute | solution.py:180
  6.6 10.1 %collective-permute-start = (bf16[16,6,256]{2,1,0:T(8,128)(2,1)S(1)}, bf16[16,6,256]{2,1,0:T(8,128)(2,1)S(1)}, u32[]{:S(2)}, u32[]{:S(2)}) collective-permute-start(bf16[16,6,256]{2,1,0:T(8,128)(2,1)S(1)} %get-tuple-element.9), channel_id=1, source_target_pairs={{0,1},{1,2},{2,3},{4,5},{5,6},{6,7},{8,9},{9,10},{10,11},{12,13},{... | collective-permute-start | bytes 147464 | tf_op jit(solution)/shard_map/ppermute | solution.py:180
  9.7 9.9 %collective-permute-start.4 = (bf16[16,6,256]{2,1,0:T(8,128)(2,1)S(1)}, bf16[16,6,256]{2,1,0:T(8,128)(2,1)S(1)}, u32[]{:S(2)}, u32[]{:S(2)}) collective-permute-start(bf16[16,6,256]{2,1,0:T(8,128)(2,1)S(1)} %get-tuple-element.8), channel_id=1, source_target_pairs={{5,0},{6,1},{7,2},{9,4},{10,5},{11,6},{13,8},{14,9},{15,10},{21,16... | collective-permute-start | bytes 147464 | tf_op jit(solution)/shard_map/ppermute | solution.py:180
  11.6 5.9 %collective-permute-start.1 = (bf16[16,6,256]{2,1,0:T(8,128)(2,1)S(1)}, bf16[16,6,256]{2,1,0:T(8,128)(2,1)S(1)}, u32[]{:S(2)}, u32[]{:S(2)}) collective-permute-start(bf16[16,6,256]{2,1,0:T(8,128)(2,1)S(1)} %get-tuple-element.8), channel_id=1, source_target_pairs={{1,0},{2,1},{3,2},{5,4},{6,5},{7,6},{9,8},{10,9},{11,10},{13,12},{... | collective-permute-start | bytes 147464 | tf_op jit(solution)/shard_map/ppermute | solution.py:180
  15.2 0.7 copy-start.3
  89.3 0.9 copy-start

commit v3 on v2

--- a/solution.py
+++ b/solution.py
@@ -19,39 +19,39 @@
 LANES = 128
 EDGE = 8
 SPAN = 2 * RADIUS + 1
-
-
-def shifted(halves, amount, lane):
+GROUP = 4
+MANY = 8
+
+
+def shifted(halves, turn, from_lower, from_upper):
     count = len(halves)
-    source = lane - amount
-    turned = [pltpu.roll(half, lax.rem(amount + LANES, LANES), 1) for half in halves]
+    turned = [pltpu.roll(half, turn, 1) for half in halves]
     blank = jnp.zeros_like(turned[0])
-    inside = (source >= 0) & (source < LANES)
     results = []
     for k in range(count):
         lower = turned[k - 1] if k > 0 else blank
         upper = turned[k + 1] if k + 1 < count else blank
-        wrapped = jnp.where(source < 0, lower, upper)
-        results.append(jnp.where(inside, turned[k], wrapped))
+        results.append(jnp.where(from_lower, lower, jnp.where(from_upper, upper, turned[k])))
     return results
 
 
 def flow_kernel(
-    center_ref, other_ref, forward_ref, ahead_ref, center, other, turned, spill, score_f, score_b, top_f, top_b
+    center_ref, other_ref, forward_ref, ahead_ref, center, turned, score_f, top_f, top_b
 ):
     channels, padded_rows, breadth = center_ref.shape
     parts = breadth // LANES
     height = padded_rows - 2 * EDGE
     other_rows = other_ref.shape[1]
     lane = lax.broadcasted_iota(jnp.int32, (8, LANES), 1)
+    many = math.gcd(height // 8, MANY)
+    together = math.gcd(channels, 16)
     factor = score_scale * math.log2(math.e)
 
     @pl.loop(0, channels)
     def _(c):
         for k in range(parts):
             cols = slice(k * LANES, (k + 1) * LANES)
-            center[c, k] = center_ref[c, :, cols].astype(jnp.float32) * factor
-            other[c, k] = other_ref[c, :, cols].astype(jnp.float32)
+            center[c, k, 0:padded_rows, :] = center_ref[c, :, cols].astype(jnp.float32) * factor
 
     top_f[...] = jnp.full(top_f.shape, -jnp.inf, jnp.float32)
     top_b[...] = jnp.full(top_b.shape, -jnp.inf, jnp.float32)
@@ -59,13 +59,22 @@
     @pl.loop(0, SPAN)
     def _(col):
         shift = col - RADIUS
-        long_lane = lax.broadcasted_iota(jnp.int32, (other_rows, LANES), 1)
-
-        @pl.loop(0, channels)
-        def _(c):
-            moved = shifted([other[c, k] for k in range(parts)], -shift, long_lane)
+        back_turn = lax.rem(LANES + shift, LANES)
+        back_masks = (lane - shift < 0, lane - shift >= LANES)
+        source = lax.broadcasted_iota(jnp.int32, (breadth, breadth), 0)
+        target = lax.broadcasted_iota(jnp.int32, (breadth, breadth), 1)
+        mover = jnp.where(source - target == shift, 1.0, 0.0).astype(jnp.bfloat16)
+
+        @pl.loop(0, channels // together)
+        def _(group):
+            these = pl.ds(group * together, together)
+            moved = jnp.dot(
+                other_ref[these].reshape(together * other_rows, breadth),
+                mover,
+                preferred_element_type=jnp.float32,
+            ).reshape(together, other_rows, breadth)
             for k in range(parts):
-                turned[c, k] = moved[k]
+                turned[these, k] = moved[:, :, k * LANES : (k + 1) * LANES]
 
         @pl.loop(0, padded_rows // 16)
         def _(pair):
@@ -73,72 +82,131 @@
             for k in range(parts):
                 sums = [[None] * SPAN for _ in range(2)]
                 for c in range(channels):
-                    mine = [center[c, k, pl.ds(base + 8 * j, 8), :] for j in range(2)]
-                    for offset in range(SPAN + 8):
-                        window = turned[c, k, pl.ds(base + EDGE - RADIUS + offset, 8), :]
-                        for j in range(2):
-                            row = offset - 8 * j
-                            if 0 <= row < SPAN:
-                                term = mine[j] * window
-                                sums[j][row] = term if c == 0 else sums[j][row] + term
+                    mine = {}
+                    windows = {}
+                    for j in range(2):
+                        for row in range(SPAN):
+                            near = (RADIUS - (row - RADIUS)) % GROUP
+                            far = 8 * j + EDGE + row - RADIUS + near
+                            if (j, near) not in mine:
+                                mine[j, near] = center[c, k, pl.ds(base + 8 * j + near, 8), :]
+                            if far not in windows:
+                                windows[far] = turned[c, k, pl.ds(base + far, 8), :]
+                            term = mine[j, near] * windows[far]
+                            sums[j][row] = term if c == 0 else sums[j][row] + term
                 for j in range(2):
                     for row in range(SPAN):
-                        spill[row, k, pl.ds(base + 8 * j, 8), :] = sums[j][row]
-
-        @pl.loop(0, height // 8)
-        def _(block):
-            base = pl.multiple_of(block * 8, 8)
-            here = pl.ds(base, 8)
-            best_f = [top_f[k, here, :] for k in range(parts)]
-            best_b = [top_b[k, here, :] for k in range(parts)]
-            for row in range(SPAN):
+                        near = (RADIUS - (row - RADIUS)) % GROUP
+                        score_f[col, row, k, pl.ds(base + 8 * j + near, 8), :] = sums[j][row]
+
+        @pl.loop(0, height // (8 * many))
+        def _(chunk):
+            raw = []
+            for j in range(many):
+                base = pl.multiple_of(chunk * (8 * many) + 8 * j, 8)
+                here = pl.ds(base, 8)
+                bests_f, bests_b = [None] * parts, [None] * parts
                 for k in range(parts):
-                    value = spill[row, k, pl.ds(base + EDGE, 8), :]
-                    score_f[col, row, k, here, :] = value
-                    best_f[k] = jnp.maximum(best_f[k], value)
-                back = shifted(
-                    [spill[row, k, pl.ds(base + EDGE + RADIUS - row, 8), :] for k in range(parts)],
-                    shift,
-                    lane,
-                )
+                    for row in range(SPAN):
+                        value = score_f[col, row, k, pl.ds(base + EDGE, 8), :]
+                        other = score_f[col, row, k, pl.ds(base + EDGE + RADIUS - row, 8), :]
+                        bests_f[k] = value if row == 0 else jnp.maximum(bests_f[k], value)
+                        bests_b[k] = other if row == 0 else jnp.maximum(bests_b[k], other)
+                    top_f[k, here, :] = jnp.maximum(top_f[k, here, :], bests_f[k])
+                raw.append((here, bests_b))
+            turned_back = [(here, shifted(values, back_turn, *back_masks)) for here, values in raw]
+            for here, values in turned_back:
                 for k in range(parts):
-                    score_b[col, row, k, here, :] = back[k]
-                    best_b[k] = jnp.maximum(best_b[k], back[k])
+                    top_b[k, here, :] = jnp.maximum(top_b[k, here, :], values[k])
+
+    @pl.loop(0, height // (8 * many))
+    def _(chunk):
+        bases = [pl.multiple_of(chunk * (8 * many) + 8 * j, 8) for j in range(many)]
+        bests_f = [[top_f[k, pl.ds(base, 8), :] for k in range(parts)] for base in bases]
+        bests_b = [[top_b[k, pl.ds(base, 8), :] for k in range(parts)] for base in bases]
+
+        def sums_of(scores, best, sign):
+            weights = [jnp.exp2(score - best) for score in scores]
+            summed = weights[RADIUS]
+            lean = None
+            for step in range(1, RADIUS + 1):
+                up, down = weights[RADIUS + step], weights[RADIUS - step]
+                summed = summed + (up + down)
+                part = (up - down) * (sign * step)
+                lean = part if lean is None else lean + part
+            return summed, lean
+
+        def one_column(col, carry):
+            shift = col - RADIUS
+            place = shift.astype(jnp.float32)
+            forth_turn = lax.rem(LANES - shift, LANES)
+            back_turn = lax.rem(LANES + shift, LANES)
+            forth_masks = (lane + shift < 0, lane + shift >= LANES)
+            back_masks = (lane - shift < 0, lane - shift >= LANES)
+            moved = [shifted(best, forth_turn, *forth_masks) for best in bests_b]
+            forward = [
+                [
+                    sums_of(
+                        [score_f[col, row, k, pl.ds(base + EDGE, 8), :] for row in range(SPAN)],
+                        bests_f[j][k],
+                        1.0,
+                    )
+                    for k in range(parts)
+                ]
+                for j, base in enumerate(bases)
+            ]
+            back = [
+                [
+                    sums_of(
+                        [
+                            score_f[col, row, k, pl.ds(base + EDGE + RADIUS - row, 8), :]
+                            for row in range(SPAN)
+                        ],
+                        moved[j][k],
+                        -1.0,
+                    )
+                    for k in range(parts)
+                ]
+                for j, base in enumerate(bases)
+            ]
+            turned_back = [
+                [shifted([value[i] for value in row], back_turn, *back_masks) for i in range(2)]
+                for row in back
+            ]
+            results = []
+            for j in range(many):
+                for k in range(parts):
+                    column = lane + (k * LANES - shift)
+                    inside = (column >= 0) & (column < breadth)
+                    outside = float(SPAN) * jnp.exp2(-bests_b[j][k])
+                    summed = jnp.where(inside, turned_back[j][0][k], outside)
+                    lean = jnp.where(inside, turned_back[j][1][k], 0.0)
+                    old = carry[j * parts + k]
+                    ahead_sum, ahead_lean = forward[j][k]
+                    results.append(
+                        (
+                            old[0] + ahead_sum,
+                            old[1] + ahead_lean,
+                            old[2] + ahead_sum * place,
+                            old[3] + summed,
+                            old[4] + lean,
+                            old[5] - summed * place,
+                        )
+                    )
+            return tuple(results)
+
+        zero = jnp.zeros((8, LANES), jnp.float32)
+        results = lax.fori_loop(0, SPAN, one_column, ((zero,) * 6,) * (many * parts))
+        for j, base in enumerate(bases):
             for k in range(parts):
-                top_f[k, here, :] = best_f[k]
-                top_b[k, here, :] = best_b[k]
-
-    for score, top, out_ref, sign in (
-        (score_f, top_f, forward_ref, 1.0),
-        (score_b, top_b, ahead_ref, -1.0),
-    ):
-
-        @pl.loop(0, height // 8)
-        def _(block):
-            here = pl.ds(pl.multiple_of(block * 8, 8), 8)
-            for k in range(parts):
-                best = top[k, here, :]
-
-                def one_column(col, carry):
-                    total, along_rows, along_cols = carry
-                    weights = [jnp.exp2(score[col, row, k, here, :] - best) for row in range(SPAN)]
-                    summed = weights[RADIUS]
-                    lean = None
-                    for step in range(1, RADIUS + 1):
-                        up, down = weights[RADIUS + step], weights[RADIUS - step]
-                        summed = summed + (up + down)
-                        part = (up - down) * float(step)
-                        lean = part if lean is None else lean + part
-                    place = (col - RADIUS).astype(jnp.float32)
-                    return total + summed, along_rows + lean, along_cols + summed * place
-
-                zero = jnp.zeros((8, LANES), jnp.float32)
-                total, along_rows, along_cols = lax.fori_loop(
-                    0, SPAN, one_column, (zero, zero, zero)
-                )
                 cols = slice(k * LANES, (k + 1) * LANES)
-                out_ref[0, here, cols] = sign * along_rows / total
-                out_ref[1, here, cols] = sign * along_cols / total
+                sums = results[j * parts + k]
+                for out_ref, (total, along_rows, along_cols) in (
+                    (forward_ref, sums[:3]),
+                    (ahead_ref, sums[3:]),
+                ):
+                    out_ref[0, pl.ds(base, 8), cols] = along_rows / total
+                    out_ref[1, pl.ds(base, 8), cols] = along_cols / total
 
 
 def flows_between(center, other):
@@ -154,12 +222,9 @@
         in_specs=[vmem, vmem],
         out_specs=(vmem, vmem),
         scratch_shapes=[
-            pltpu.VMEM((channels, parts, padded_rows, LANES), jnp.float32),
+            pltpu.VMEM((channels, parts, padded_rows + 8, LANES), jnp.float32),
             pltpu.VMEM((channels, parts, other_rows, LANES), jnp.float32),
-            pltpu.VMEM((channels, parts, other_rows, LANES), jnp.float32),
-            pltpu.VMEM((SPAN, parts, padded_rows, LANES), jnp.float32),
-            pltpu.VMEM((SPAN, SPAN, parts, height, LANES), jnp.float32),
-            pltpu.VMEM((SPAN, SPAN, parts, height, LANES), jnp.float32),
+            pltpu.VMEM((SPAN, SPAN, parts, padded_rows + 8, LANES), jnp.float32),
             pltpu.VMEM((parts, height, LANES), jnp.float32),
             pltpu.VMEM((parts, height, LANES), jnp.float32),
         ],

time: 116 us -> 77.8 us (0.67)
  Pallas kernels: 94.4 us -> 55.7 us
    pallas_call x1, Pallas kernels: 69.2 us -> 30.6 us  [flows_between(): pl.pallas_call(flow_kernel, out_shape=(shape, shape), in_specs=[vmem, vme...]
  transfers between devices with their start and end apart: 5 -> 5, of which waited for: 1 -> 1; matrix products, arithmetic and copies ran while one was open for 4% -> 6% of each run, Pallas kernels for 0% -> 0%
where the time goes in v3:
time: 77.8 us; the launch traced here: 77.4 us
  Pallas kernels  55.7 us (72%)
  starting transfers between devices  11.9 us (15%)
  local copies, waits for them, and re-layouts  6.39 us (8%)
  between operations  1.44 us (2%)
  other arithmetic  1.08 us (1%)
  waiting for transfers between devices  0.83 us (1%)
    pallas_call x1, Pallas kernels, flows_between(): pl.pallas_call(flow_kernel, out_shape=(shape, shape), in_specs=[vmem, vme...  30.6 us
    pallas_call x1, Pallas kernels, relaxed(): pl.pallas_call(relax_kernel, out_shape=jax.ShapeDtypeStruct(pair, jnp.flo...  25.2 us
    ppermute x5, starting transfers between devices, sent(): return lax.ppermute(value, axes, pairs)  11.9 us
    concatenate x2, local copies, waits for them, and re-layouts, margins(): return jnp.concatenate([blank, before, middle, after, blank], axis=1)  2.55 us
    unnamed x9, local copies, waits for them, and re-layouts  2.21 us
  transfers between devices with their start and end apart: 5, of which 1 were waited for; matrix products, arithmetic and copies ran while one was open for 6% of the time, Pallas kernels for 0%

profile of v3, /device:TPU:9, one launch (start us, length us, event | category | flops | bytes accessed | tf_op | source)
XLA Modules:
  0.0 77.4 jit_solution(17181405150616795063)
XLA Ops:
  0.6 1.9 %collective-permute-start.3 = (bf16[16,64,256]{2,1,0:T(8,128)(2,1)}, bf16[16,64,256]{2,1,0:T(8,128)(2,1)S(1)}, u32[]{:S(2)}, u32[]{:S(2)}) collective-permute-start(bf16[16,64,256]{2,1,0:T(8,128)(2,1)} %bitcast.8), channel_id=1, source_target_pairs={{4,0},{5,1},{6,2},{7,3},{8,4},{9,5},{10,6},{11,7},{12,8},{13,9},{1... | collective-permute-start | bytes 1572872 | tf_op jit(solution)/shard_map/ppermute | solution.py:245
  2.6 0.0 copy-start.2
  2.6 0.9 %fusion.1 = (bf16[16,6,256]{2,1,0:T(8,128)(2,1)S(1)}, bf16[16,6,256]{2,1,0:T(8,128)(2,1)S(1)}) fusion(bf16[16,64,256]{2,1,0:T(8,128)(2,1)} %bitcast.9), kind=kLoop, calls=%fused_computation.7 | loop fusion | bytes 196608 | tf_op jit(solution)/shard_map/slice | solution.py:579
  3.5 0.0 copy-start.1
  3.5 3.1 %collective-permute-start.2 = (bf16[16,6,256]{2,1,0:T(8,128)(2,1)S(1)}, bf16[16,6,256]{2,1,0:T(8,128)(2,1)S(1)}, u32[]{:S(2)}, u32[]{:S(2)}) collective-permute-start(bf16[16,6,256]{2,1,0:T(8,128)(2,1)S(1)} %get-tuple-element.9), channel_id=1, source_target_pairs={{4,1},{5,2},{6,3},{8,5},{9,6},{10,7},{12,9},{13,10},{14,11},{20,17... | collective-permute-start | bytes 147464 | tf_op jit(solution)/shard_map/ppermute | solution.py:245
  6.6 3.1 %collective-permute-start = (bf16[16,6,256]{2,1,0:T(8,128)(2,1)S(1)}, bf16[16,6,256]{2,1,0:T(8,128)(2,1)S(1)}, u32[]{:S(2)}, u32[]{:S(2)}) collective-permute-start(bf16[16,6,256]{2,1,0:T(8,128)(2,1)S(1)} %get-tuple-element.9), channel_id=1, source_target_pairs={{0,1},{1,2},{2,3},{4,5},{5,6},{6,7},{8,9},{9,10},{10,11},{12,13},{... | collective-permute-start | bytes 147464 | tf_op jit(solution)/shard_map/ppermute | solution.py:245
  9.7 1.9 %collective-permute-start.4 = (bf16[16,6,256]{2,1,0:T(8,128)(2,1)S(1)}, bf16[16,6,256]{2,1,0:T(8,128)(2,1)S(1)}, u32[]{:S(2)}, u32[]{:S(2)}) collective-permute-start(bf16[16,6,256]{2,1,0:T(8,128)(2,1)S(1)} %get-tuple-element.8), channel_id=1, source_target_pairs={{5,0},{6,1},{7,2},{9,4},{10,5},{11,6},{13,8},{14,9},{15,10},{21,16... | collective-permute-start | bytes 147464 | tf_op jit(solution)/shard_map/ppermute | solution.py:245
  11.6 1.9 %collective-permute-start.1 = (bf16[16,6,256]{2,1,0:T(8,128)(2,1)S(1)}, bf16[16,6,256]{2,1,0:T(8,128)(2,1)S(1)}, u32[]{:S(2)}, u32[]{:S(2)}) collective-permute-start(bf16[16,6,256]{2,1,0:T(8,128)(2,1)S(1)} %get-tuple-element.8), channel_id=1, source_target_pairs={{1,0},{2,1},{3,2},{5,4},{6,5},{7,6},{9,8},{10,9},{11,10},{13,12},{... | collective-permute-start | bytes 147464 | tf_op jit(solution)/shard_map/ppermute | solution.py:245
  13.5 0.0 copy-done.2
  13.5 0.2 fusion
  13.7 0.1 slice_reduce_fusion
  13.8 0.1 maximum_multiply_fusion
  13.9 0.6 fusion.2
  15.2 0.0 copy-start.3
  15.2 0.0 copy-done.1
  15.2 0.6 copy-done.3
  15.8 0.1 select_reduce_fusion.stiff_ref
  15.9 0.7 pad_maximum_fusion.links_ref
  16.7 0.0 collective-permute-done
  16.7 0.8 %collective-permute-done.1 = bf16[16,6,256]{2,1,0:T(8,128)(2,1)S(1)} collective-permute-done((bf16[16,6,256]{2,1,0:T(8,128)(2,1)S(1)}, bf16[16,6,256]{2,1,0:T(8,128)(2,1)S(1)}, u32[]{:S(2)}, u32[]{:S(2)}) %collective-permute-start.1) | collective-permute-done | bytes 49184 | tf_op jit(solution)/shard_map/ppermute | solution.py:245
  17.5 2.0 %concatenate.10.center_ref = bf16[16,80,256]{2,1,0:T(8,128)(2,1)S(1)} concatenate(bf16[16,2,256]{2,1,0:T(2,128)(2,1)S(1)} %broadcast_in_dim.26, bf16[16,6,256]{2,1,0:T(8,128)(2,1)S(1)} %collective-permute-done, bf16[16,64,256]{2,1,0:T(8,128)(2,1)} %bitcast.10, bf16[16,6,256]{2,1,0:T(8,128)(2,1)S(1)} %collective-permute-done.1, bf16[16,2,256]{2,1,0:T(2,128)(2,1)S(1)} %broadcast_in_dim.26), dimensions={1} | concatenate | bytes 1310720 | tf_op jit(solution)/shard_map/concatenate | solution.py:251
  19.5 0.0 collective-permute-done.2
  19.5 0.0 collective-permute-done.4
  19.5 0.0 collective-permute-done.3
  19.6 0.5 concatenate.11.other_ref
  20.1 30.6 %shard_map.59 = (f32[2,64,256]{2,1,0:T(8,128)}, f32[2,64,256]{2,1,0:T(8,128)S(1)}) custom-call(bf16[16,80,256]{2,1,0:T(8,128)(2,1)S(1)} %concatenate.10.center_ref, bf16[16,96,256]{2,1,0:T(8,128)(2,1)S(1)} %concatenate.11.other_ref), custom_call_target="tpu_custom_call" | custom-call | tf_op jit(solution)/shard_map/pallas_call | solution.py:219
  50.7 0.0 copy-start
  50.7 0.9 %copy-done = f32[2,64,256]{2,1,0:T(8,128)S(1)} copy-done((f32[2,64,256]{2,1,0:T(8,128)S(1)}, f32[2,64,256]{2,1,0:T(8,128)}, u32[]{:S(2)}) %copy-start) | copy-done | bytes 131096
  51.6 25.2 %shard_map.60 = f32[2,64,256]{2,1,0:T(8,128)S(1)} custom-call(f32[2]{0:T(128)S(1)} %pad_maximum_fusion.links_ref, f32[2,64,256]{2,1,0:T(8,128)S(1)} %copy-done, f32[2,64,256]{2,1,0:T(8,128)S(1)} %get-tuple-element.5.ahead_ref, f32[64,256]{1,0:T(8,128)S(1)} %select_reduce_fusion.stiff_ref), custom_call_target="tpu_custom_call" | custom-call | tf_op jit(solution)/shard_map/pallas_call | solution.py:539
  76.8 0.7 copy.7
  (2 shorter events, 0.0 us)
Async XLA Ops:
  0.6 18.9 %collective-permute-start.3 = (bf16[16,64,256]{2,1,0:T(8,128)(2,1)}, bf16[16,64,256]{2,1,0:T(8,128)(2,1)S(1)}, u32[]{:S(2)}, u32[]{:S(2)}) collective-permute-start(bf16[16,64,256]{2,1,0:T(8,128)(2,1)} %bitcast.8), channel_id=1, source_target_pairs={{4,0},{5,1},{6,2},{7,3},{8,4},{9,5},{10,6},{11,7},{12,8},{13,9},{1... | collective-permute-start | bytes 1572872 | tf_op jit(solution)/shard_map/ppermute | solution.py:245
  2.6 11.0 %copy-start.2 = (s32[4,4]{1,0:T(4,128)S(1)}, s32[4,4]{1,0:T(4,128)}, u32[]{:S(2)}) copy-start(s32[4,4]{1,0:T(4,128)} %param.7) | copy-start | bytes 196
  3.5 11.7 %copy-start.1 = (s32[1,64,256]{2,1,0:T(8,128)S(1)}, s32[1,64,256]{2,1,0:T(8,128)}, u32[]{:S(2)}) copy-start(s32[1,64,256]{2,1,0:T(8,128)} %param.5) | copy-start | bytes 196612
  3.5 16.0 %collective-permute-start.2 = (bf16[16,6,256]{2,1,0:T(8,128)(2,1)S(1)}, bf16[16,6,256]{2,1,0:T(8,128)(2,1)S(1)}, u32[]{:S(2)}, u32[]{:S(2)}) collective-permute-start(bf16[16,6,256]{2,1,0:T(8,128)(2,1)S(1)} %get-tuple-element.9), channel_id=1, source_target_pairs={{4,1},{5,2},{6,3},{8,5},{9,6},{10,7},{12,9},{13,10},{14,11},{20,17... | collective-permute-start | bytes 147464 | tf_op jit(solution)/shard_map/ppermute | solution.py:245
  6.6 10.1 %collective-permute-start = (bf16[16,6,256]{2,1,0:T(8,128)(2,1)S(1)}, bf16[16,6,256]{2,1,0:T(8,128)(2,1)S(1)}, u32[]{:S(2)}, u32[]{:S(2)}) collective-permute-start(bf16[16,6,256]{2,1,0:T(8,128)(2,1)S(1)} %get-tuple-element.9), channel_id=1, source_target_pairs={{0,1},{1,2},{2,3},{4,5},{5,6},{6,7},{8,9},{9,10},{10,11},{12,13},{... | collective-permute-start | bytes 147464 | tf_op jit(solution)/shard_map/ppermute | solution.py:245
  9.7 9.9 %collective-permute-start.4 = (bf16[16,6,256]{2,1,0:T(8,128)(2,1)S(1)}, bf16[16,6,256]{2,1,0:T(8,128)(2,1)S(1)}, u32[]{:S(2)}, u32[]{:S(2)}) collective-permute-start(bf16[16,6,256]{2,1,0:T(8,128)(2,1)S(1)} %get-tuple-element.8), channel_id=1, source_target_pairs={{5,0},{6,1},{7,2},{9,4},{10,5},{11,6},{13,8},{14,9},{15,10},{21,16... | collective-permute-start | bytes 147464 | tf_op jit(solution)/shard_map/ppermute | solution.py:245
  11.6 5.9 %collective-permute-start.1 = (bf16[16,6,256]{2,1,0:T(8,128)(2,1)S(1)}, bf16[16,6,256]{2,1,0:T(8,128)(2,1)S(1)}, u32[]{:S(2)}, u32[]{:S(2)}) collective-permute-start(bf16[16,6,256]{2,1,0:T(8,128)(2,1)S(1)} %get-tuple-element.8), channel_id=1, source_target_pairs={{1,0},{2,1},{3,2},{5,4},{6,5},{7,6},{9,8},{10,9},{11,10},{13,12},{... | collective-permute-start | bytes 147464 | tf_op jit(solution)/shard_map/ppermute | solution.py:245
  15.2 0.7 copy-start.3
  50.7 0.9 %copy-start = (f32[2,64,256]{2,1,0:T(8,128)S(1)}, f32[2,64,256]{2,1,0:T(8,128)}, u32[]{:S(2)}) copy-start(f32[2,64,256]{2,1,0:T(8,128)} %get-tuple-element.4.forward_ref) | copy-start | bytes 393220

commit v4 on v3

--- a/solution.py
+++ b/solution.py
@@ -269,6 +269,7 @@
     summed_in,
     above,
     below,
+    excess,
     rounded,
     above_in,
     below_in,
@@ -313,10 +314,18 @@
         for step in range(STEPS):
             for part in range(2):
                 disp[step, part, edge, :] = jnp.zeros((EDGE, breadth), jnp.float32)
-    for array in (prior, backward, summed_in):
-        array[...] = jnp.zeros(array.shape, array.dtype)
-    above_in[...] = jnp.zeros(above_in.shape, above_in.dtype)
-    below_in[...] = jnp.zeros(below_in.shape, below_in.dtype)
+    for absent, arrays in (
+        (section == 0, (prior, backward, below_in)),
+        (section < 2, (summed_in,)),
+        (section == sections - 1, (above_in,)),
+    ):
+
+        @pl.when(absent)
+        def _():
+            for array in arrays:
+                array[...] = jnp.zeros(array.shape, array.dtype)
+
+    excess[...] = link_here * (forward_ref[...] - ahead_ref[...])
     stiff[EDGE : EDGE + height, :] = stiff_ref[...]
 
     barrier = pltpu.get_barrier_semaphore()
@@ -356,21 +365,20 @@
         def _():
             copy.wait_recv()
 
-    flows = []
-    for part in range(2):
-        pieces = []
-        for which, (source, target) in enumerate(((forward_ref, prior), (ahead_ref, backward))):
-            pieces.append(
-                send(
-                    has_next,
-                    source.at[part],
-                    target.at[part],
-                    flow_send.at[part, which],
-                    flow_recv.at[part, which],
-                    next_section,
-                )
+    terms, flows = [
+        [
+            send(
+                has_next,
+                source.at[part],
+                target.at[part],
+                flow_send.at[part, which],
+                flow_recv.at[part, which],
+                next_section,
             )
-        flows.append(pieces)
+            for part in range(2)
+        ]
+        for which, (source, target) in enumerate(((excess, backward), (forward_ref, prior)))
+    ]
     stiff_down = send(
         has_next_tile, stiff.at[last], stiff.at[top], stiff_send.at[0], stiff_recv.at[0], next_tile
     )
@@ -398,8 +406,7 @@
         return down, up
 
     for part in range(2):
-        for copy in flows[part]:
-            arrive(has_prior, copy)
+        arrive(has_prior, terms[part])
         chain = pltpu.make_async_remote_copy(
             src_ref=summed.at[part],
             dst_ref=summed_in.at[part],
@@ -410,7 +417,7 @@
         )
         arrive(section > 1, chain)
         before = summed_in[part]
-        here = before + link_below * (prior[part] - backward[part])
+        here = before + backward[part]
         summed[part] = here
         send(
             has_next & has_prior,
@@ -422,9 +429,12 @@
         )
         disp[0, part, EDGE : EDGE + height, :] = 0.5 * here
         below[part] = 0.5 * before
-        above[part] = 0.5 * (here + link_here * (forward_ref[part] - ahead_ref[part]))
+        above[part] = 0.5 * (here + excess[part])
 
     rows = send_rows(0)
+    for part in range(2):
+        arrive(has_prior, flows[part])
+        backward[part] = prior[part] - backward[part]
     arrive(has_prior_tile, stiff_down)
     arrive(has_next_tile, stiff_up)
     lane = lax.broadcasted_iota(jnp.int32, (16, breadth), 1)
@@ -544,7 +554,7 @@
         scratch_shapes=[
             pltpu.VMEM((height + 2 * EDGE, breadth), jnp.float32),
             pltpu.VMEM((STEPS, 2, height + 2 * EDGE, breadth), jnp.float32),
-            *[pltpu.VMEM(pair, jnp.float32) for _ in range(6)],
+            *[pltpu.VMEM(pair, jnp.float32) for _ in range(7)],
             *[pltpu.VMEM(moved, jnp.bfloat16) for _ in range(3)],
             dma((2, 2)),
             dma((2, 2)),

time: 77.8 us -> 77.8 us (level)
  no operation moved by 1% of the time
where the time goes in v4:
time: 77.8 us; the launch traced here: 77.4 us
  Pallas kernels  55.7 us (72%)
  starting transfers between devices  11.9 us (15%)
  local copies, waits for them, and re-layouts  6.39 us (8%)
  between operations  1.44 us (2%)
  other arithmetic  1.08 us (1%)
  waiting for transfers between devices  0.83 us (1%)
    pallas_call x1, Pallas kernels, flows_between(): pl.pallas_call(flow_kernel, out_shape=(shape, shape), in_specs=[vmem, vme...  30.6 us
    pallas_call x1, Pallas kernels, relaxed(): pl.pallas_call(relax_kernel, out_shape=jax.ShapeDtypeStruct(pair, jnp.flo...  25.2 us
    ppermute x5, starting transfers between devices, sent(): return lax.ppermute(value, axes, pairs)  11.9 us
    concatenate x2, local copies, waits for them, and re-layouts, margins(): return jnp.concatenate([blank, before, middle, after, blank], axis=1)  2.55 us
    unnamed x9, local copies, waits for them, and re-layouts  2.21 us
  transfers between devices with their start and end apart: 5, of which 1 were waited for; matrix products, arithmetic and copies ran while one was open for 6% of the time, Pallas kernels for 0%

profile of v4, /device:TPU:9, one launch (start us, length us, event | category | flops | bytes accessed | tf_op | source)
XLA Modules:
  0.0 77.4 jit_solution(18445249477638538782)
XLA Ops:
  0.6 1.9 %collective-permute-start.3 = (bf16[16,64,256]{2,1,0:T(8,128)(2,1)}, bf16[16,64,256]{2,1,0:T(8,128)(2,1)S(1)}, u32[]{:S(2)}, u32[]{:S(2)}) collective-permute-start(bf16[16,64,256]{2,1,0:T(8,128)(2,1)} %bitcast.8), channel_id=1, source_target_pairs={{4,0},{5,1},{6,2},{7,3},{8,4},{9,5},{10,6},{11,7},{12,8},{13,9},{1... | collective-permute-start | bytes 1572872 | tf_op jit(solution)/shard_map/ppermute | solution.py:245
  2.6 0.0 copy-start.2
  2.6 0.9 %fusion.1 = (bf16[16,6,256]{2,1,0:T(8,128)(2,1)S(1)}, bf16[16,6,256]{2,1,0:T(8,128)(2,1)S(1)}) fusion(bf16[16,64,256]{2,1,0:T(8,128)(2,1)} %bitcast.9), kind=kLoop, calls=%fused_computation.7 | loop fusion | bytes 196608 | tf_op jit(solution)/shard_map/slice | solution.py:589
  3.5 0.0 copy-start.1
  3.5 3.1 %collective-permute-start.2 = (bf16[16,6,256]{2,1,0:T(8,128)(2,1)S(1)}, bf16[16,6,256]{2,1,0:T(8,128)(2,1)S(1)}, u32[]{:S(2)}, u32[]{:S(2)}) collective-permute-start(bf16[16,6,256]{2,1,0:T(8,128)(2,1)S(1)} %get-tuple-element.9), channel_id=1, source_target_pairs={{4,1},{5,2},{6,3},{8,5},{9,6},{10,7},{12,9},{13,10},{14,11},{20,17... | collective-permute-start | bytes 147464 | tf_op jit(solution)/shard_map/ppermute | solution.py:245
  6.6 3.1 %collective-permute-start = (bf16[16,6,256]{2,1,0:T(8,128)(2,1)S(1)}, bf16[16,6,256]{2,1,0:T(8,128)(2,1)S(1)}, u32[]{:S(2)}, u32[]{:S(2)}) collective-permute-start(bf16[16,6,256]{2,1,0:T(8,128)(2,1)S(1)} %get-tuple-element.9), channel_id=1, source_target_pairs={{0,1},{1,2},{2,3},{4,5},{5,6},{6,7},{8,9},{9,10},{10,11},{12,13},{... | collective-permute-start | bytes 147464 | tf_op jit(solution)/shard_map/ppermute | solution.py:245
  9.7 1.9 %collective-permute-start.4 = (bf16[16,6,256]{2,1,0:T(8,128)(2,1)S(1)}, bf16[16,6,256]{2,1,0:T(8,128)(2,1)S(1)}, u32[]{:S(2)}, u32[]{:S(2)}) collective-permute-start(bf16[16,6,256]{2,1,0:T(8,128)(2,1)S(1)} %get-tuple-element.8), channel_id=1, source_target_pairs={{5,0},{6,1},{7,2},{9,4},{10,5},{11,6},{13,8},{14,9},{15,10},{21,16... | collective-permute-start | bytes 147464 | tf_op jit(solution)/shard_map/ppermute | solution.py:245
  11.6 1.9 %collective-permute-start.1 = (bf16[16,6,256]{2,1,0:T(8,128)(2,1)S(1)}, bf16[16,6,256]{2,1,0:T(8,128)(2,1)S(1)}, u32[]{:S(2)}, u32[]{:S(2)}) collective-permute-start(bf16[16,6,256]{2,1,0:T(8,128)(2,1)S(1)} %get-tuple-element.8), channel_id=1, source_target_pairs={{1,0},{2,1},{3,2},{5,4},{6,5},{7,6},{9,8},{10,9},{11,10},{13,12},{... | collective-permute-start | bytes 147464 | tf_op jit(solution)/shard_map/ppermute | solution.py:245
  13.5 0.0 copy-done.2
  13.5 0.2 fusion
  13.7 0.1 slice_reduce_fusion
  13.8 0.1 maximum_multiply_fusion
  13.9 0.6 fusion.2
  15.2 0.0 copy-start.3
  15.2 0.0 copy-done.1
  15.2 0.6 copy-done.3
  15.8 0.1 select_reduce_fusion.stiff_ref
  15.9 0.7 pad_maximum_fusion.links_ref
  16.7 0.0 collective-permute-done
  16.7 0.8 %collective-permute-done.1 = bf16[16,6,256]{2,1,0:T(8,128)(2,1)S(1)} collective-permute-done((bf16[16,6,256]{2,1,0:T(8,128)(2,1)S(1)}, bf16[16,6,256]{2,1,0:T(8,128)(2,1)S(1)}, u32[]{:S(2)}, u32[]{:S(2)}) %collective-permute-start.1) | collective-permute-done | bytes 49184 | tf_op jit(solution)/shard_map/ppermute | solution.py:245
  17.5 2.0 %concatenate.10.center_ref = bf16[16,80,256]{2,1,0:T(8,128)(2,1)S(1)} concatenate(bf16[16,2,256]{2,1,0:T(2,128)(2,1)S(1)} %broadcast_in_dim.26, bf16[16,6,256]{2,1,0:T(8,128)(2,1)S(1)} %collective-permute-done, bf16[16,64,256]{2,1,0:T(8,128)(2,1)} %bitcast.10, bf16[16,6,256]{2,1,0:T(8,128)(2,1)S(1)} %collective-permute-done.1, bf16[16,2,256]{2,1,0:T(2,128)(2,1)S(1)} %broadcast_in_dim.26), dimensions={1} | concatenate | bytes 1310720 | tf_op jit(solution)/shard_map/concatenate | solution.py:251
  19.5 0.0 collective-permute-done.2
  19.5 0.0 collective-permute-done.4
  19.5 0.0 collective-permute-done.3
  19.6 0.5 concatenate.11.other_ref
  20.1 30.6 %shard_map.59 = (f32[2,64,256]{2,1,0:T(8,128)}, f32[2,64,256]{2,1,0:T(8,128)S(1)}) custom-call(bf16[16,80,256]{2,1,0:T(8,128)(2,1)S(1)} %concatenate.10.center_ref, bf16[16,96,256]{2,1,0:T(8,128)(2,1)S(1)} %concatenate.11.other_ref), custom_call_target="tpu_custom_call" | custom-call | tf_op jit(solution)/shard_map/pallas_call | solution.py:219
  50.7 0.0 copy-start
  50.7 0.9 %copy-done = f32[2,64,256]{2,1,0:T(8,128)S(1)} copy-done((f32[2,64,256]{2,1,0:T(8,128)S(1)}, f32[2,64,256]{2,1,0:T(8,128)}, u32[]{:S(2)}) %copy-start) | copy-done | bytes 131096
  51.6 25.2 %shard_map.60 = f32[2,64,256]{2,1,0:T(8,128)S(1)} custom-call(f32[2]{0:T(128)S(1)} %pad_maximum_fusion.links_ref, f32[2,64,256]{2,1,0:T(8,128)S(1)} %copy-done, f32[2,64,256]{2,1,0:T(8,128)S(1)} %get-tuple-element.5.ahead_ref, f32[64,256]{1,0:T(8,128)S(1)} %select_reduce_fusion.stiff_ref), custom_call_target="tpu_custom_call" | custom-call | tf_op jit(solution)/shard_map/pallas_call | solution.py:549
  76.7 0.7 copy.7
  (2 shorter events, 0.0 us)
Async XLA Ops:
  0.6 18.9 %collective-permute-start.3 = (bf16[16,64,256]{2,1,0:T(8,128)(2,1)}, bf16[16,64,256]{2,1,0:T(8,128)(2,1)S(1)}, u32[]{:S(2)}, u32[]{:S(2)}) collective-permute-start(bf16[16,64,256]{2,1,0:T(8,128)(2,1)} %bitcast.8), channel_id=1, source_target_pairs={{4,0},{5,1},{6,2},{7,3},{8,4},{9,5},{10,6},{11,7},{12,8},{13,9},{1... | collective-permute-start | bytes 1572872 | tf_op jit(solution)/shard_map/ppermute | solution.py:245
  2.6 11.0 %copy-start.2 = (s32[4,4]{1,0:T(4,128)S(1)}, s32[4,4]{1,0:T(4,128)}, u32[]{:S(2)}) copy-start(s32[4,4]{1,0:T(4,128)} %param.7) | copy-start | bytes 196
  3.5 11.7 %copy-start.1 = (s32[1,64,256]{2,1,0:T(8,128)S(1)}, s32[1,64,256]{2,1,0:T(8,128)}, u32[]{:S(2)}) copy-start(s32[1,64,256]{2,1,0:T(8,128)} %param.5) | copy-start | bytes 196612
  3.5 16.0 %collective-permute-start.2 = (bf16[16,6,256]{2,1,0:T(8,128)(2,1)S(1)}, bf16[16,6,256]{2,1,0:T(8,128)(2,1)S(1)}, u32[]{:S(2)}, u32[]{:S(2)}) collective-permute-start(bf16[16,6,256]{2,1,0:T(8,128)(2,1)S(1)} %get-tuple-element.9), channel_id=1, source_target_pairs={{4,1},{5,2},{6,3},{8,5},{9,6},{10,7},{12,9},{13,10},{14,11},{20,17... | collective-permute-start | bytes 147464 | tf_op jit(solution)/shard_map/ppermute | solution.py:245
  6.6 10.1 %collective-permute-start = (bf16[16,6,256]{2,1,0:T(8,128)(2,1)S(1)}, bf16[16,6,256]{2,1,0:T(8,128)(2,1)S(1)}, u32[]{:S(2)}, u32[]{:S(2)}) collective-permute-start(bf16[16,6,256]{2,1,0:T(8,128)(2,1)S(1)} %get-tuple-element.9), channel_id=1, source_target_pairs={{0,1},{1,2},{2,3},{4,5},{5,6},{6,7},{8,9},{9,10},{10,11},{12,13},{... | collective-permute-start | bytes 147464 | tf_op jit(solution)/shard_map/ppermute | solution.py:245
  9.7 9.9 %collective-permute-start.4 = (bf16[16,6,256]{2,1,0:T(8,128)(2,1)S(1)}, bf16[16,6,256]{2,1,0:T(8,128)(2,1)S(1)}, u32[]{:S(2)}, u32[]{:S(2)}) collective-permute-start(bf16[16,6,256]{2,1,0:T(8,128)(2,1)S(1)} %get-tuple-element.8), channel_id=1, source_target_pairs={{5,0},{6,1},{7,2},{9,4},{10,5},{11,6},{13,8},{14,9},{15,10},{21,16... | collective-permute-start | bytes 147464 | tf_op jit(solution)/shard_map/ppermute | solution.py:245
  11.6 5.9 %collective-permute-start.1 = (bf16[16,6,256]{2,1,0:T(8,128)(2,1)S(1)}, bf16[16,6,256]{2,1,0:T(8,128)(2,1)S(1)}, u32[]{:S(2)}, u32[]{:S(2)}) collective-permute-start(bf16[16,6,256]{2,1,0:T(8,128)(2,1)S(1)} %get-tuple-element.8), channel_id=1, source_target_pairs={{1,0},{2,1},{3,2},{5,4},{6,5},{7,6},{9,8},{10,9},{11,10},{13,12},{... | collective-permute-start | bytes 147464 | tf_op jit(solution)/shard_map/ppermute | solution.py:245
  15.2 0.7 copy-start.3
  50.7 0.9 %copy-start = (f32[2,64,256]{2,1,0:T(8,128)S(1)}, f32[2,64,256]{2,1,0:T(8,128)}, u32[]{:S(2)}) copy-start(f32[2,64,256]{2,1,0:T(8,128)} %get-tuple-element.4.forward_ref) | copy-start | bytes 393220
